TPU v7x, 32 devices: a whole 2x2x4 slice. The times are simulated.
32 devices in a mesh: dp: 8 (over y, x, core), fsdp: 4 (over z).
Axes of the slice: x: 2, y: 2, z: 4, core: 2. Of those that a mesh axis runs over, the one named last changes fastest.
Arguments:
- tokens: bfloat16 [16384, 768], P(('dp', 'fsdp')), may hold values from -6 to 6
- coarse_view: bfloat16 [4096, 768], P(('dp', 'fsdp')), may hold values from -6 to 6
- segment_ids: int32 [32, 512], P(('dp', 'fsdp')), may hold values from 0 to 2, as said below
- partner_device: int32 [128, 1], P(('dp', 'fsdp')), may hold values from 0 to 7; in each aligned block of 4 rows (0 to 3, 4 to 7, ...) at most 2 rows name the same one
- partner_slot: int32 [128], P(('dp', 'fsdp')), may hold values from 0 to 3
- mix_weight: float32 [128], P(('dp', 'fsdp')), may hold values from 0.25 to 0.75
- ln1_gain: bfloat16 [768], P(('dp', 'fsdp')), may hold values from 0.5 to 1.5
- w_qkv: bfloat16 [768, 2304], P(None, ('dp', 'fsdp')), may hold values from -0.21875 to 0.21875
- w_out: bfloat16 [768, 768], P(('dp', 'fsdp')), may hold values from -3.5 to 3.5
- lnx_gain: bfloat16 [768], P(('dp', 'fsdp')), may hold values from 0.5 to 1.5
- w_cq: bfloat16 [768, 768], P(('dp', 'fsdp')), may hold values from -0.21875 to 0.21875
- w_ckv: bfloat16 [768, 1536], P(None, ('dp', 'fsdp')), may hold values from -0.21875 to 0.21875
- w_cout: bfloat16 [768, 768], P(('dp', 'fsdp')), may hold values from -3.5 to 3.5
- ln2_gain: bfloat16 [768], P(('dp', 'fsdp')), may hold values from 0.5 to 1.5
- w_up: bfloat16 [768, 3072], P(None, ('dp', 'fsdp')), may hold values from -0.21875 to 0.21875
- w_down: bfloat16 [3072, 768], P(('dp', 'fsdp')), may hold values from -0.109375 to 0.109375
- cotangent: bfloat16 [16384, 768], P(('dp', 'fsdp')), may hold values from -6 to 6
Outputs:
- output: bfloat16 [16384, 768], P(('dp', 'fsdp'))
- token_grad: float32 [16384, 768], P(('dp', 'fsdp'))
- coarse_grad: float32 [4096, 768], P(('dp', 'fsdp'))
- ln1_grad: float32 [768], P(('dp', 'fsdp'))
- qkv_grad: float32 [768, 2304], P(None, ('dp', 'fsdp'))
- out_grad: float32 [768, 768], P(('dp', 'fsdp'))
- lnx_grad: float32 [768], P(('dp', 'fsdp'))
- cq_grad: float32 [768, 768], P(('dp', 'fsdp'))
- ckv_grad: float32 [768, 1536], P(None, ('dp', 'fsdp'))
- cout_grad: float32 [768, 768], P(('dp', 'fsdp'))
- ln2_grad: float32 [768], P(('dp', 'fsdp'))
- up_grad: float32 [768, 3072], P(None, ('dp', 'fsdp'))
- down_grad: float32 [3072, 768], P(('dp', 'fsdp'))
Inputs may be any that keep to these rules, and one draw needn't show every extreme that they name: `partner_device`: among the 4 blocks of one device no value appears more than 2 times, and some device has a value exactly 2 times. `segment_ids`: ids never fall along a device's row; each device holds three videos, each a whole number of mixup blocks of 128 tokens, the longest exactly 256 tokens.
All inputs are finite; a program needn't handle non-finite values.
Results may differ from a plain program's by a relative error of at most 0.02.
Values may be sent and summed in bfloat16 or wider, within the bound.
No kernel may reach another device: no remote copies, remote signals or barrier semaphores. Data moves between devices by JAX's collectives and lax.ppermute only.
A program may use at most 256 MiB of HBM per device.

v0:
```python
import functools

import jax
import jax.numpy as jnp
from jax import lax
from jax.experimental import pallas as pl
from jax.experimental.pallas import tpu as pltpu
from jax.sharding import PartitionSpec as P

HEADS = 12
HEAD = 64
PAIR = 2 * HEAD
CORE = 1
CLIP = 128
WINDOW = 256
TILE = 256
f32 = jnp.float32
bf16 = jnp.bfloat16
fence = lax.optimization_barrier


def swap(values, mask):
    count = lax.axis_size("dp")
    return lax.ppermute(values, "dp", [(i, i ^ mask) for i in range(count)])


def shift(values, step):
    count = lax.axis_size("fsdp")
    return lax.ppermute(values, "fsdp", [(i, (i + step) % count) for i in range(count)])


def link_masks():
    masks = []
    mask = 2
    while mask < lax.axis_size("dp"):
        masks.append(mask)
        mask *= 2
    return masks


def inner_swap(values, mask):
    count = lax.axis_size("fsdp")
    return lax.ppermute(values, "fsdp", [(i, i ^ mask) for i in range(count)])


def inner_double(held, mask):
    return inner_join(held, inner_swap(held, mask), mask)


def inner_join(held, came, mask):
    high = (lax.axis_index("fsdp") & mask) != 0
    return jnp.concatenate([jnp.where(high, came, held), jnp.where(high, held, came)])


def inner_rest(held):
    while held.shape[0] < lax.axis_size("fsdp"):
        held = inner_double(held, held.shape[0])
    return held


def inner_start(shard):
    return [shard] + [shift(shard, step) for step in range(1, lax.axis_size("fsdp"))]


def inner_order(came):
    count = len(came)
    me = lax.axis_index("fsdp")
    line = [came[count - 1 - k] for k in range(count)] + [came[count - k] for k in range(1, count)]
    return lax.dynamic_slice_in_dim(jnp.stack(line), count - 1 - me, count, 0)


def mirrored(role):
    masks = link_masks()
    return sum(masks[len(masks) - 1 - i] for i, mask in enumerate(masks) if role & mask)


def step_along(values, mask):
    count = lax.axis_size("dp")
    return lax.ppermute(values, "dp", [(i, i ^ (mirrored(mask) if i & CORE else mask)) for i in range(count)])


def top_bit(role):
    return 1 << (role.bit_length() - 1)


def relayed_roles():
    found = [role for role in range(2, lax.axis_size("dp"), 2) if role & (role - 1)]
    return sorted(found, key=lambda role: bin(role).count("1"))


def device_of(me, role, mirrors):
    holder = me ^ (role & CORE)
    link = role & ~CORE
    return holder ^ (link + lax.rem(holder, 2) * (mirrors[link] - link))


def mirror_table():
    return {role: mirrored(role) for role in range(0, lax.axis_size("dp"), 2)}


def single_steps(block):
    return {mask: step_along(block, mask) for mask in link_masks()}


def relay_steps(held):
    for role in relayed_roles():
        held[role] = step_along(held[role ^ top_bit(role)], top_bit(role))


def parts_of(pieces, total):
    return [pieces[e] for e in sorted(pieces)], tuple((e, 0, total) for e in sorted(pieces))


def core_steps(held):
    return {**held, **{e | CORE: swap(block, CORE) for e, block in held.items()}}


def inner_parts(inner):
    inner.add()
    return inner.parts


def add_low(a, b):
    return (a.astype(f32) + b.astype(f32)).astype(bf16)


class OuterSum:
    def __init__(self, *parts):
        self.parts = {2 * g: [part[g] for part in parts] for g in range(lax.axis_size("dp") // 2)}
        self.came = []
        self.ready = {}

    def prepare(self, role, rows=slice(None)):
        self.ready[role, rows.start] = self.value(role, rows).astype(bf16)

    def going(self, role, rows):
        return self.ready[role, rows.start] if (role, rows.start) in self.ready else self.value(role, rows).astype(bf16)

    def value(self, role, rows=slice(None)):
        total = self.parts[role][0][rows].astype(f32)
        for part in self.parts[role][1:]:
            total = total + part[rows].astype(f32)
        return total

    def relays(self):
        for role in relayed_roles()[::-1]:
            came = step_along(self.value(role).astype(bf16), top_bit(role))
            self.parts[role ^ top_bit(role)].append(came)

    def singles(self, rows=slice(None), masks=None):
        self.came.append((rows, [step_along(self.going(mask, rows), mask) for mask in masks or link_masks()]))

    def result(self, index=None):
        found = {}
        for rows, blocks in self.came:
            found.setdefault(rows.start, (rows, []))[1].extend(blocks)
        chosen = list(found.values())
        sums = []
        for rows, blocks in chosen if index is None else [chosen[index]]:
            total = self.value(0, rows)
            for block in blocks:
                total = total + block.astype(f32)
            sums.append(total)
        return sums[0] if len(sums) == 1 else jnp.concatenate(sums)

    def state(self):
        return (self.parts, [blocks for _, blocks in self.came], list(self.ready.values()))

    def put(self, state):
        self.parts = state[0]
        self.ready = dict(zip(self.ready, state[2]))
        self.came = [(rows, blocks) for (rows, _), blocks in zip(self.came, state[1])]


class InnerSum:
    def __init__(self, parts):
        self.parts = parts
        self.came = None
        self.mask = parts.shape[0]

    def step(self):
        self.add()
        self.mask //= 2
        bit = ((lax.axis_index("fsdp") & self.mask) != 0).astype(jnp.int32)
        halves = self.parts.reshape((2, self.mask) + self.parts.shape[1:])
        self.parts = lax.dynamic_index_in_dim(halves, bit, 0, keepdims=False)
        going = lax.dynamic_index_in_dim(halves, 1 - bit, 0, keepdims=False).astype(bf16)
        self.came = inner_swap(going, self.mask)

    def finish(self, steps=None):
        while self.mask > 1:
            self.step()

    def add(self):
        if self.came is not None:
            self.parts = self.parts + self.came.astype(f32)
            self.came = None

    def result(self):
        self.finish()
        self.add()
        return self.parts[0]


def nn(a, b):
    return jnp.dot(a, b, preferred_element_type=f32)


def nt(a, b):
    return lax.dot_general(a, b, (((1,), (1,)), ((), ())), preferred_element_type=f32)


def tn(a, b):
    return lax.dot_general(a, b, (((0,), (0,)), ((), ())), preferred_element_type=f32)


def tiles(size):
    step = TILE if size % TILE == 0 else size
    return [(at, step) for at in range(0, size, step)]


def centred(values):
    centre = jnp.mean(values, axis=-1, keepdims=True)
    shifted = values - centre
    spread = jnp.mean(shifted * shifted, axis=-1, keepdims=True)
    r = lax.rsqrt(spread + 1e-06)
    return shifted * r, r


def norm_back(xhat, r, gain, grad):
    c = grad * gain
    first = jnp.mean(c, axis=-1, keepdims=True)
    second = jnp.mean(c * xhat, axis=-1, keepdims=True)
    return r * (c - first - xhat * second), jnp.sum(grad * xhat, axis=0, keepdims=True)


def lower_half(rows):
    return lax.broadcasted_iota(jnp.int32, (rows, PAIR), 1) < HEAD


def two_heads(rows):
    keep = lower_half(rows.shape[0])
    zero = jnp.zeros_like(rows)
    return jnp.concatenate([jnp.where(keep, rows, zero), jnp.where(keep, zero, rows)], axis=0)


def side_by_side(stacked):
    rows = stacked.shape[0] // 2
    return jnp.where(lower_half(rows), stacked[:rows], stacked[rows:])


def softmax_rows(scores):
    raised = jnp.exp(scores - jnp.max(scores, axis=-1, keepdims=True))
    return raised / jnp.sum(raised, axis=-1, keepdims=True)


def bias_of(key_seg, own_seg):
    return jnp.where(key_seg == own_seg, 0.0, -1e30).astype(f32)


def block_bias(key_seg, ints, blocks):
    return jnp.stack([bias_of(key_seg[...], ints[1 + 3 * blocks + i]) for i in range(blocks)])


def biased(scores, bias):
    blocks, _, keys = bias.shape
    rows = scores.shape[0] // (2 * blocks)
    return (scores.reshape(2, blocks, rows, keys) + bias[None]).reshape(scores.shape)


def copies(jobs, sems, at):
    made = [pltpu.make_async_copy(src, dst, sems.at[at + i]) for i, (src, dst) in enumerate(jobs)]
    for job in made:
        job.start()
    return made


def whole(shape, dtype):
    return jax.ShapeDtypeStruct(shape, dtype)


VMEM = pl.BlockSpec(memory_space=pltpu.VMEM)
SMEM = pl.BlockSpec(memory_space=pltpu.SMEM)
ANY = pl.BlockSpec(memory_space=pl.ANY)


def params(mib=56):
    return pltpu.CompilerParams(vmem_limit_bytes=mib * 1024 * 1024)


def cost(flops, moved, exps=0):
    return pl.CostEstimate(flops=int(flops), bytes_accessed=int(moved), transcendentals=int(exps))


def first_kernel(
    geometry, ints, mix, seg_row, tokens, *refs
):
    dp_count, blocks, token_places, qkv_places, qkv_rows, mirrors = geometry
    n_tok, n_qkv = len(token_places), len(qkv_places)
    token_refs, qkv_refs = refs[:n_tok], refs[n_tok : n_tok + n_qkv]
    blended_ref, qkv_ref, attended_ref, gains_ref, partner, weight, gain_parts, sems = refs[n_tok + n_qkv :]
    me = ints[0]
    width = tokens.shape[1]

    for b in range(blocks):
        holder, slot = ints[1 + b], ints[1 + blocks + b]
        for ref, (role, _, rows) in zip(token_refs, token_places):

            @pl.when(holder == device_of(me, role, mirrors))
            def _(ref=ref, rows=rows, b=b, slot=slot):
                at = pl.multiple_of(slot * CLIP, CLIP)
                pltpu.make_async_copy(ref.at[pl.ds(at, CLIP)], partner.at[b], sems.at[b]).start()

    jobs = []
    for ref, (e, start, rows) in zip(qkv_refs, qkv_places):
        take = min(rows, qkv_rows - start)
        at = pl.multiple_of(device_of(me, e, mirrors) * qkv_rows + start, 16)
        jobs.append((ref.at[pl.ds(0, take)], weight.at[pl.ds(at, take)]))
        if start + rows > qkv_rows:
            jobs.append((ref.at[pl.ds(take, rows - take)], gain_parts.at[e]))
    made = copies(jobs, sems, blocks)
    for b in range(blocks):
        pltpu.make_async_copy(tokens.at[pl.ds(0, CLIP)], partner.at[b], sems.at[b]).wait()
    for b in range(blocks):
        rows = slice(b * CLIP, (b + 1) * CLIP)
        share = mix[b]
        blended_ref[rows, :] = share * tokens[rows, :].astype(f32) + (1.0 - share) * partner[b].astype(f32)
    for job in made:
        job.wait()
    gains = gain_parts[0].astype(f32)
    for e in range(1, dp_count):
        gains = gains + gain_parts[e].astype(f32)
    gains_ref[...] = gains[:8]
    xhat, _ = centred(blended_ref[...])
    normed = (xhat * gains[0:1]).astype(bf16)
    for at, step in tiles(3 * width):
        tile = nt(normed, weight[at : at + step, :])
        if at + step <= width:
            tile = tile * 0.125
        qkv_ref[:, at : at + step] = tile.astype(bf16)

    @pl.loop(0, blocks)
    def _(i):
        window = pl.multiple_of(ints[1 + 2 * blocks + i] * CLIP, CLIP)
        bias = bias_of(seg_row[:, pl.ds(window, WINDOW)], ints[1 + 3 * blocks + i])
        rows = pl.ds(pl.multiple_of(i * CLIP, CLIP), CLIP)
        keys = pl.ds(window, WINDOW)
        for at in range(0, width, PAIR):
            queries = two_heads(qkv_ref[rows, at : at + PAIR])
            probs = softmax_rows(nt(queries, qkv_ref[keys, width + at : width + at + PAIR]) + bias).astype(bf16)
            out = nn(probs, qkv_ref[keys, 2 * width + at : 2 * width + at + PAIR])
            attended_ref[rows, at : at + PAIR] = side_by_side(out).astype(bf16)


def load_cross(me, refs, places, layout, weights, sems, mirrors):
    jobs = []
    for ref, (e, start, rows) in zip(refs, places):
        for (first, size), weight in zip(layout, weights):
            if weight is not None and first >= start and first + size <= start + rows:
                at = pl.multiple_of(device_of(me, e, mirrors) * size, 16)
                jobs.append((ref.at[pl.ds(first - start, size)], weight.at[pl.ds(at, size)]))
    return copies(jobs, sems, 0)


def second_kernel(geometry, ints, coarse_seg, coarse, blended, attended, gains, *refs):
    blocks, places, layout, mirrors = geometry
    weight_refs = refs[: len(places)]
    residual_ref, cq_ref, ckv_ref, crossed_ref, joined_ref, second_ref = refs[len(places) : len(places) + 6]
    w_ckv, w_out, w_cq, w_cout, sems = refs[len(places) + 6 :]
    made = load_cross(ints[0], weight_refs, places, layout, (w_ckv, w_out, w_cq, w_cout), sems, mirrors)
    for job in made:
        job.wait()
    width = blended.shape[1]
    for at, step in tiles(2 * width):
        ckv_ref[:, at : at + step] = nt(coarse[...], w_ckv[at : at + step, :]).astype(bf16)
    for at, step in tiles(width):
        residual_ref[:, at : at + step] = blended[:, at : at + step] + nn(attended[...], w_out[:, at : at + step])
    xhat, _ = centred(residual_ref[...])
    crossed_in = (xhat * gains[1:2]).astype(bf16)
    for at, step in tiles(width):
        cq_ref[:, at : at + step] = (nn(crossed_in, w_cq[:, at : at + step]) * 0.125).astype(bf16)

    bias = block_bias(coarse_seg, ints, blocks)
    for at in range(0, width, PAIR):
        queries = two_heads(cq_ref[:, at : at + PAIR])
        probs = softmax_rows(biased(nt(queries, ckv_ref[:, at : at + PAIR]), bias)).astype(bf16)
        out = nn(probs, ckv_ref[:, width + at : width + at + PAIR])
        crossed_ref[:, at : at + PAIR] = side_by_side(out).astype(bf16)

    for at, step in tiles(width):
        joined_ref[:, at : at + step] = residual_ref[:, at : at + step] + nn(crossed_ref[...], w_cout[:, at : at + step])
    xhat, _ = centred(joined_ref[...])
    second_ref[...] = (xhat * gains[2:3]).astype(bf16)


def mlp_kernel(geometry, second, second_near, cotangent, cotangent_near, *refs):
    groups, places, rows, last = geometry
    weight_refs = refs[: len(places)]
    refs = refs[len(places) :]
    keep_ref, going_ref = refs[:2]
    if last:
        own_ref = refs[2]
        sums = refs[3:7]
        refs = refs[7:]
    else:
        sums = refs[2:6]
        refs = refs[6:]
    w_up, w_down, hidden, grad_pre, sems = refs
    step = pl.program_id(0)

    def jobs_of(group):
        jobs = []
        for ref, (e, which) in zip(weight_refs, places):
            if e == groups[group]:
                for part, weight in ((0, w_up), (1, w_down)):
                    if which is None or which == part:
                        first = part * rows if which is None else 0
                        jobs.append((ref.at[pl.ds(first, rows)], weight.at[group]))
        return jobs

    at = 0
    for group in range(len(groups)):
        jobs = jobs_of(group)
        made = [pltpu.make_async_copy(s, d, sems.at[at + i]) for i, (s, d) in enumerate(jobs)]
        at += len(jobs)

        @pl.when(step == 0)
        def _(made=made):
            for job in made:
                job.start()

        @pl.when(step == group)
        def _(made=made):
            for job in made:
                job.wait()

    @pl.when(step == 0)
    def _():
        for ref in sums:
            ref[...] = jnp.zeros_like(ref)

    up, down = w_up.at[step], w_down.at[step]
    for half, (inputs, upstream) in enumerate(((second, cotangent), (second_near, cotangent_near))):
        pre = nt(inputs[...], up[...])
        grad_hidden = nt(upstream[...], down[...])
        cdf = 0.5 * (1.0 + lax.erf(pre * 0.7071067811865476))
        slope = cdf + pre * (jnp.exp(-0.5 * pre * pre) * 0.3989422804014327)
        hidden[half] = (pre * cdf).astype(bf16)
        grad_pre[half] = (grad_hidden * slope).astype(bf16)
        for first, size in tiles(second.shape[1]):
            columns = slice(first, first + size)
            sums[2 * half][:, columns] += nn(hidden[half], down[:, columns])
            sums[2 * half + 1][:, columns] += nn(grad_pre[half], up[:, columns])
    keep_ref[0, 0] = (tn(grad_pre[0], second[...]) + tn(grad_pre[1], second_near[...])).astype(bf16)
    keep_ref[0, 1] = (tn(hidden[0], cotangent[...]) + tn(hidden[1], cotangent_near[...])).astype(bf16)

    @pl.when(step == len(groups) - 1)
    def _():
        going_ref[0] = sums[2][...].astype(bf16)
        going_ref[1] = sums[3][...].astype(bf16)
        if last:
            own_ref[0] = sums[0][...].astype(bf16)
            own_ref[1] = sums[1][...].astype(bf16)


def grads_out(me, dp_count, layout, sources, keep_ref, send_ref, sems, at, mirrors):
    jobs = []
    for e in range(dp_count):
        target = send_ref if e & CORE else keep_ref
        for (first, size), source in zip(layout, sources):
            if source is None:
                continue
            row = pl.multiple_of(device_of(me, e, mirrors) * size, 16)
            jobs.append((source.at[pl.ds(row, size)], target.at[e // 2, pl.ds(first, size)]))
    return copies(jobs, sems, at)


def third_kernel(
    geometry, ints, coarse_seg, gains, mlp_out, grad_second, own_b, came_a, came_b, joined, cotangent, crossed, cq, ckv, *refs
):
    blocks, places, layout, dp_count, mirrors = geometry
    weight_refs = refs[: len(places)]
    refs = refs[len(places) :]
    output_ref, grad_joined_ref, grad_cq_ref, grad_ckv_ref, gain_grads_ref, keep_ref, send_ref = refs[:7]
    w_cout, g_cout, grad_cross, sems = refs[7:]
    me = ints[0]
    width = joined.shape[1]
    made = load_cross(me, weight_refs, places, layout, (None, None, None, w_cout), sems, mirrors)
    rest = [own_b[i].astype(f32) + came_a[i].astype(f32) + came_b[i].astype(f32) for i in range(2)]
    output_ref[...] = (joined[...] + (mlp_out[...] + rest[0])).astype(bf16)
    xhat, r = centred(joined[...])
    grad_in, gain_two = norm_back(xhat, r, gains[2:3], grad_second[...] + rest[1])
    grad_joined_ref[...] = cotangent[...].astype(f32) + grad_in
    low = grad_joined_ref[...].astype(bf16)
    for job in made:
        job.wait()
    for at, step in tiles(width):
        grad_cross[:, at : at + step] = nt(low, w_cout[at : at + step, :]).astype(bf16)
    for at, step in tiles(width):
        g_cout[at : at + step, :] = tn(crossed[:, at : at + step], low).astype(bf16)
    going = grads_out(me, dp_count, layout, (None, None, None, g_cout), keep_ref, send_ref, sems, len(made), mirrors)
    bias = block_bias(coarse_seg, ints, blocks)
    for at in range(0, width, PAIR):
        lanes = slice(at, at + PAIR)
        queries = two_heads(cq[:, lanes])
        grads = two_heads(grad_cross[:, lanes])
        keys = ckv[:, lanes]
        values = ckv[:, width + at : width + at + PAIR]
        probs = softmax_rows(biased(nt(queries, keys), bias))
        grad_ckv_ref[:, width + at : width + at + PAIR] = tn(probs.astype(bf16), grads).astype(bf16)
        grad_probs = nt(grads, values)
        inner = jnp.sum(probs * grad_probs, axis=-1, keepdims=True)
        scores = (probs * (grad_probs - inner)).astype(bf16)
        part = side_by_side(nn(scores, keys)).astype(bf16)
        grad_cq_ref[:, lanes] = part * jnp.asarray(0.125, bf16)
        grad_ckv_ref[:, lanes] = tn(scores, queries).astype(bf16)

    gain_grads_ref[...] = jnp.concatenate([gain_two] * 8, axis=0)
    for job in going:
        job.wait()


def third_part(geometry, ints, coarse, gains, gain_two, grad_joined, residual, attended, grad_cq, grad_ckv, keep_in, send_in, *refs):
    places, layout, dp_count, mirrors = geometry
    weight_refs = refs[: len(places)]
    refs = refs[len(places) :]
    coarse_ref, grad_res_ref, grad_att_ref, gain_grads_ref, keep_ref, send_ref = refs[:6]
    w_ckv, w_out, w_cq, g_ckv, g_out, g_cq, crossed_in, sems = refs[6:]
    me = ints[0]
    width = residual.shape[1]
    made = load_cross(me, weight_refs, places, layout, (w_ckv, w_out, w_cq, None), sems, mirrors)
    xhat, r = centred(residual[...])
    crossed_in[...] = (xhat * gains[1:2]).astype(bf16)
    for at, step in tiles(width):
        g_cq[at : at + step, :] = tn(crossed_in[:, at : at + step], grad_cq[...]).astype(bf16)
    for at, step in tiles(2 * width):
        g_ckv[at : at + step, :] = tn(grad_ckv[:, at : at + step], coarse[...]).astype(bf16)
    for job in made:
        job.wait()
    going = grads_out(me, dp_count, layout, (g_ckv, None, g_cq, None), keep_ref, send_ref, sems, 0, mirrors)
    for at, step in tiles(width):
        coarse_ref[:, at : at + step] = nn(grad_ckv[:, 0:width], w_ckv[0:width, at : at + step]) + nn(
            grad_ckv[:, width : 2 * width], w_ckv[width : 2 * width, at : at + step]
        )
    pieces = [nt(grad_cq[...], w_cq[at : at + step, :]) for at, step in tiles(width)]
    grad_in, gain_cross = norm_back(xhat, r, gains[1:2], jnp.concatenate(pieces, axis=1))
    grad_res = grad_joined[...] + grad_in
    grad_res_ref[...] = grad_res
    low = grad_res.astype(bf16)
    for at, step in tiles(width):
        g_out[at : at + step, :] = tn(attended[:, at : at + step], low).astype(bf16)
    going += grads_out(me, dp_count, layout, (None, g_out, None, None), keep_ref, send_ref, sems, len(going), mirrors)
    for at, step in tiles(width):
        grad_att_ref[:, at : at + step] = nt(low, w_out[at : at + step, :]).astype(bf16)
    zero = jnp.zeros_like(gain_cross)
    gain_grads_ref[...] = jnp.concatenate([zero, gain_cross, gain_two[0:1]] + [zero] * 5, axis=0)
    for job in going:
        job.wait()


def fourth_kernel(geometry, ints, seg_row, grad_att, qkv, *refs):
    blocks, first, last = geometry
    count = last - first
    grad_proj, sems = refs[-1 - 5 * count - 1], refs[-1]
    scratch = refs[-1 - 5 * count : -1]
    query_part, key_part, value_part, key_sum, value_sum = [scratch[i * count : (i + 1) * count] for i in range(5)]
    width = grad_att.shape[1]
    for ref in key_sum + value_sum:
        ref[...] = jnp.zeros_like(ref)

    @pl.loop(0, blocks)
    def _(i):
        window = pl.multiple_of(ints[1 + 2 * blocks + i] * CLIP, CLIP)
        bias = bias_of(seg_row[:, pl.ds(window, WINDOW)], ints[1 + 3 * blocks + i])
        rows = pl.ds(pl.multiple_of(i * CLIP, CLIP), CLIP)
        near = pl.ds(window, WINDOW)
        for pair in range(count):
            at = (first + pair) * PAIR
            queries = two_heads(qkv[rows, at : at + PAIR])
            grads = two_heads(grad_att[rows, at : at + PAIR])
            keys = qkv[near, width + at : width + at + PAIR]
            values = qkv[near, 2 * width + at : 2 * width + at + PAIR]
            probs = softmax_rows(nt(queries, keys) + bias)
            grad_probs = nt(grads, values)
            inner = jnp.sum(probs * grad_probs, axis=-1, keepdims=True)
            scores = (probs * (grad_probs - inner)).astype(bf16)
            part = side_by_side(nn(scores, keys)).astype(bf16)
            query_part[pair][rows, :] = part * jnp.asarray(0.125, bf16)
            value_sum[pair][near, :] += tn(probs.astype(bf16), grads)
            key_sum[pair][near, :] += tn(scores, queries)

    jobs = []
    for pair in range(count):
        key_part[pair][...] = key_sum[pair][...].astype(bf16)
        value_part[pair][...] = value_sum[pair][...].astype(bf16)
        for i, part in enumerate((query_part, key_part, value_part)):
            jobs.append((part[pair], grad_proj.at[:, pl.ds(i * width + (first + pair) * PAIR, PAIR)]))
    for job in copies(jobs, sems, 0):
        job.wait()


def fifth_kernel(geometry, ints, mix, gains, blended, grad_res, grad_proj, *refs):
    dp_count, blocks, qkv_places, qkv_rows, mirrors = geometry
    weight_refs = refs[: len(qkv_places)]
    refs = refs[len(qkv_places) :]
    base_ref, going_ref = refs[:2]
    weight, sems = refs[2:]
    me = ints[0]
    width = blended.shape[1]
    jobs = []
    for ref, (e, start, rows) in zip(weight_refs, qkv_places):
        take = min(rows, qkv_rows - start)
        at = pl.multiple_of(device_of(me, e, mirrors) * qkv_rows + start, 16)
        jobs.append((ref.at[pl.ds(0, take)], weight.at[pl.ds(at, take)]))
    made = copies(jobs, sems, 0)
    xhat, r = centred(blended[...])
    for job in made:
        job.wait()
    pieces = [nn(grad_proj[...], weight[:, at : at + step]) for at, step in tiles(width)]
    grad_in, _ = norm_back(xhat, r, gains[0:1], jnp.concatenate(pieces, axis=1))
    grad_blend = grad_res[...] + grad_in
    for b in range(blocks):
        rows = slice(b * CLIP, (b + 1) * CLIP)
        share = mix[b]
        part = grad_blend[rows, :]
        base_ref[rows, :] = share * part
        going_ref[rows, :] = ((1.0 - share) * part).astype(bf16)


def place_kernel(geometry, ints, ints_near, blocks_own, blocks_near, out_ref):
    blocks, mirrors = geometry
    me = ints[0]
    out_ref[...] = jnp.zeros_like(out_ref)
    for table, first, source in ((ints, 1, blocks_own), (ints_near, 0, blocks_near)):
        for b in range(blocks):
            holder, slot = table[first + b], table[first + blocks + b]
            group = jnp.int32(0)
            for role in mirrors:
                group = group + jnp.where(device_of(me, role, mirrors) == holder, role // 2, 0)

            @pl.when(lax.rem(holder, 2) == lax.rem(me, 2))
            def _(group=group, slot=slot, source=source, b=b):
                rows = pl.ds(pl.multiple_of(slot * CLIP, CLIP), CLIP)
                part = source[b * CLIP : (b + 1) * CLIP, :].astype(f32)
                out_ref[group, rows, :] = (out_ref[group, rows, :].astype(f32) + part).astype(bf16)


def sixth_kernel(geometry, ints, gains, gain_grads, blended, grad_proj, *refs):
    dp_count, qkv_places, qkv_rows, mirrors = geometry
    weight_refs = refs[: len(qkv_places)]
    keep_ref, send_ref, weight, grad_w, gain_rows, sems = refs[len(qkv_places) :]
    me = ints[0]
    width = blended.shape[1]
    jobs = []
    for ref, (e, start, rows) in zip(weight_refs, qkv_places):
        take = min(rows, qkv_rows - start)
        at = pl.multiple_of(device_of(me, e, mirrors) * qkv_rows + start, 16)
        jobs.append((ref.at[pl.ds(0, take)], weight.at[pl.ds(at, take)]))
    made = copies(jobs, sems, 0)
    xhat, _ = centred(blended[...])
    normed = (xhat * gains[0:1]).astype(bf16)
    for job in made:
        job.wait()
    gain_one = jnp.zeros((1, width), f32)
    for at, step in tiles(3 * width):
        part = tn(grad_proj[:, at : at + step], normed)
        gain_one = gain_one + jnp.sum(part * weight[at : at + step, :].astype(f32), axis=0, keepdims=True)
        grad_w[at : at + step, :] = part.astype(bf16)
    sent = grads_out(me, dp_count, ((0, qkv_rows),), (grad_w,), keep_ref, send_ref, sems, len(jobs), mirrors)
    all_gains = jnp.concatenate([gain_one / gains[0:1], gain_grads[1:8], jnp.zeros((8, width), f32)], axis=0)
    gain_rows[...] = all_gains.astype(bf16)
    last = []
    for e in range(dp_count):
        target = send_ref if e & CORE else keep_ref
        last.append((gain_rows, target.at[e // 2, pl.ds(qkv_rows, 16)]))
    for job in sent + copies(last, sems, len(jobs) + dp_count):
        job.wait()


def shards(
    tokens,
    coarse_view,
    segment_ids,
    partner_device,
    partner_slot,
    mix_weight,
    ln1_gain,
    w_qkv,
    w_out,
    lnx_gain,
    w_cq,
    w_ckv,
    w_cout,
    ln2_gain,
    w_up,
    w_down,
    cotangent,
):
    row_count, width = tokens.shape
    coarse_rows = coarse_view.shape[0]
    blocks = mix_weight.shape[0]
    dp_count, fsdp_count = lax.axis_size("dp"), lax.axis_size("fsdp")
    dp_me, fsdp_me = lax.axis_index("dp"), lax.axis_index("fsdp")
    part = ln1_gain.shape[0]
    device_me = dp_me * fsdp_count + fsdp_me
    pairs = dp_count // 2
    mirrors = mirror_table()

    target = partner_device[:, 0]
    segments = segment_ids[0]
    videos = segments.reshape(blocks, row_count // blocks)[:, 0]
    following = jnp.concatenate([videos[1:] == videos[:-1], jnp.zeros((1,), bool)])
    before = jnp.concatenate([jnp.zeros((1,), bool), videos[1:] == videos[:-1]])
    index = jnp.arange(blocks, dtype=jnp.int32)
    window = jnp.where(following, index, jnp.where(before, index - 1, jnp.minimum(index, blocks - 2)))
    ints = jnp.concatenate(
        [dp_me[None].astype(jnp.int32), target, partner_slot, window, videos]
    )
    ints_near = swap(ints[1 : 1 + 2 * blocks], CORE)
    seg_row = segments[None, :]
    coarse_seg = segments.reshape(coarse_rows, row_count // coarse_rows)[:, 0][None, :]

    gain_rows = lax.dynamic_update_slice(
        jnp.zeros((8, width), bf16), jnp.stack([ln1_gain, lnx_gain, ln2_gain]), (0, device_me * part)
    )
    shard_one = jnp.concatenate([w_qkv.T, gain_rows])
    shard_first = jnp.concatenate([shard_one, w_ckv.T])
    shard_rest = jnp.concatenate([w_out, w_cq, w_cout])
    shard_mlp = jnp.concatenate([w_up.T, w_down])
    sizes_two = (w_ckv.shape[1], w_out.shape[0], w_cq.shape[0], w_cout.shape[0])
    qkv_part, up_part = w_qkv.shape[1], w_up.shape[1]
    qkv_rows, up_rows = qkv_part * fsdp_count, up_part * fsdp_count
    layout = []
    at = 0
    for size in sizes_two:
        layout.append((at * fsdp_count, size * fsdp_count))
        at += size
    layout = tuple(layout)
    rows_two = at * fsdp_count

    held_tok = {0: tokens, **single_steps(tokens)}
    came_first = inner_start(shard_first)
    held_tok, came_first, shard_rest = fence((held_tok, came_first, shard_rest))

    firsts = inner_order(came_first)
    ones = firsts[:, : qkv_part + 8]
    gain_block = jnp.sum(ones[:, qkv_part:].astype(f32), axis=0).astype(bf16)
    block_one = jnp.concatenate(
        [ones[:, :qkv_part].reshape(qkv_rows, width), gain_block, jnp.zeros((8, width), bf16)]
    )
    held_one = {0: block_one, **single_steps(block_one)}
    came_rest = inner_start(shard_rest)
    held_tok, held_one, came_rest, shard_mlp, firsts = fence((held_tok, held_one, came_rest, shard_mlp, firsts))

    near_mlp = inner_swap(shard_mlp, 1)
    core_tok = core_steps(dict(held_tok))
    near_tok = set(held_tok)
    relay_steps(held_tok)
    rests = inner_order(came_rest)
    split = [firsts[:, qkv_part + 8 :].reshape(sizes_two[0] * fsdp_count, width)]
    at = 0
    for size in sizes_two[1:]:
        split.append(rests[:, at : at + size].reshape(size * fsdp_count, width))
        at += size
    block_two = jnp.concatenate(split)
    held_one, core_tok, held_tok, block_two, near_mlp = fence((held_one, core_tok, held_tok, block_two, near_mlp))

    cuts = (0, 5 * up_part // 12, 3 * up_part // 2, 2 * up_part)
    mlp_cut = [
        inner_join(shard_mlp[None, first:last], near_mlp[None, first:last], 1) for first, last in zip(cuts, cuts[1:])
    ]
    mlp_came = [inner_swap(mlp_cut[0], 2)]
    core_one = core_steps(dict(held_one))
    relay_steps(held_one)
    late_tok = core_steps({e: b for e, b in held_tok.items() if e not in near_tok})
    held_one, core_one, late_tok, block_two, mlp_cut, mlp_came = fence(
        (held_one, core_one, late_tok, block_two, mlp_cut, mlp_came)
    )

    held_two = {0: block_two, **single_steps(block_two)}
    cotangent_near = swap(cotangent, CORE)
    mlp_came.append(inner_swap(mlp_cut[1], 2))
    mlp_joined = [inner_rest(inner_join(mlp_cut[0], mlp_came[0], 2))]
    late_one = core_steps({e: b for e, b in held_one.items() if e not in near_tok})
    pieces_tok = {**core_tok, **late_tok}
    pieces_one = {**core_one, **late_one}
    arrays_tok, places_tok = parts_of(pieces_tok, row_count)
    arrays_one, places_one = parts_of(pieces_one, qkv_rows + 16)
    blended, qkv, attended, gains = pl.pallas_call(
        functools.partial(first_kernel, (dp_count, blocks, places_tok, places_one, qkv_rows, mirrors)),
        out_shape=(
            whole((row_count, width), f32),
            whole((row_count, 3 * width), bf16),
            whole((row_count, width), bf16),
            whole((8, width), f32),
        ),
        in_specs=[SMEM, SMEM, VMEM, VMEM] + [ANY] * (len(arrays_tok) + len(arrays_one)),
        out_specs=(VMEM,) * 4,
        scratch_shapes=[
            pltpu.VMEM((blocks, CLIP, width), bf16),
            pltpu.VMEM((3 * width, width), bf16),
            pltpu.VMEM((dp_count, 16, width), bf16),
            pltpu.SemaphoreType.DMA((blocks + len(arrays_one) + dp_count,)),
        ],
        compiler_params=params(),
        cost_estimate=cost(1e9, 1e6),
        name="mix_self_attention",
    )(ints, mix_weight, seg_row, tokens, *arrays_tok, *arrays_one)
    held_two, attended, mlp_came, cotangent_near, mlp_cut, mlp_joined = fence(
        (held_two, attended, mlp_came, cotangent_near, mlp_cut, mlp_joined)
    )

    core_two = core_steps(dict(held_two))
    relay_steps(held_two)
    mlp_came.append(inner_swap(mlp_cut[2], 2))
    mlp_joined.append(inner_rest(inner_join(mlp_cut[1], mlp_came[1], 2)))
    held_two, core_two, mlp_came, mlp_joined = fence((held_two, core_two, mlp_came, mlp_joined))

    mlp_joined.append(inner_rest(inner_join(mlp_cut[2], mlp_came[2], 2)))
    mlp = jnp.concatenate(mlp_joined, axis=1)
    block_mlp = jnp.concatenate([mlp[:, :up_part].reshape(up_rows, width), mlp[:, up_part:].reshape(up_rows, width)])
    held_mlp = {0: block_mlp, **single_steps(block_mlp)}
    late_two = core_steps({e: b for e, b in held_two.items() if e not in near_tok})
    pieces_two = {**core_two, **late_two}
    wide = [pltpu.VMEM((sizes * fsdp_count * dp_count, width), bf16) for sizes in sizes_two]
    n_two = 4 * dp_count
    arrays_two, places_two = parts_of(pieces_two, rows_two)
    wide = [pltpu.VMEM((sizes * fsdp_count * dp_count, width), bf16) for sizes in sizes_two]
    n_two = 4 * dp_count
    residual, cq, ckv, crossed, joined, second = pl.pallas_call(
        functools.partial(second_kernel, (blocks, places_two, layout, mirrors)),
        out_shape=(
            whole((row_count, width), f32),
            whole((row_count, width), bf16),
            whole((coarse_rows, 2 * width), bf16),
            whole((row_count, width), bf16),
            whole((row_count, width), f32),
            whole((row_count, width), bf16),
        ),
        in_specs=[SMEM] + [VMEM] * 5 + [ANY] * len(arrays_two),
        out_specs=(VMEM,) * 6,
        scratch_shapes=wide + [pltpu.SemaphoreType.DMA((n_two,))],
        compiler_params=params(),
        cost_estimate=cost(1e9, 1e6),
        name="cross_attention",
    )(ints, coarse_seg, coarse_view, blended, attended, gains, *arrays_two)
    second_near = swap(second, CORE)
    held_mlp, second, second_near, ints_near = fence((held_mlp, second, second_near, ints_near))

    early = dict(held_mlp)
    relay_steps(held_mlp)

    def mlp_call(pieces, last):
        groups = tuple(sorted(pieces))
        count = len(groups)
        fixed = pl.BlockSpec((row_count, width), lambda g: (0, 0))
        moving = pl.BlockSpec((1, 2, up_rows, width), lambda g: (g, 0, 0, 0))
        both = pl.BlockSpec((2, row_count, width), lambda g: (0, 0, 0))
        table = whole((row_count, width), f32)
        out_shape = [whole((count, 2, up_rows, width), bf16), whole((2, row_count, width), bf16)]
        out_specs = [moving, both]
        scratch = [pltpu.VMEM((row_count, width), f32)] * (4 if last else 2)
        if last:
            out_shape.append(whole((2, row_count, width), bf16))
            out_specs.append(both)
        else:
            out_shape += [table, table]
            out_specs += [fixed, fixed]
        made = pl.pallas_call(
            functools.partial(mlp_kernel, (groups, tuple((e, None) for e in groups), up_rows, last)),
            grid=(count,),
            out_shape=tuple(out_shape),
            in_specs=[fixed] * 4 + [ANY] * count,
            out_specs=tuple(out_specs),
            scratch_shapes=scratch
            + [
                pltpu.VMEM((count, up_rows, width), bf16),
                pltpu.VMEM((count, up_rows, width), bf16),
                pltpu.VMEM((2, row_count, up_rows), bf16),
                pltpu.VMEM((2, row_count, up_rows), bf16),
                pltpu.SemaphoreType.DMA((2 * count,)),
            ],
            compiler_params=params(32),
            cost_estimate=cost(1e9, 1e6),
            name="feed_forward",
        )(second, second_near, cotangent, cotangent_near, *[pieces[e] for e in groups])
        return groups, made[0].reshape(count, 2 * up_rows, width), made[1], made[2:]

    groups_a, keep_a, going_a, (mlp_out, grad_second) = mlp_call(early, False)
    late = {e: b for e, b in held_mlp.items() if e not in near_tok}
    late, keep_a, going_a, mlp_out, grad_second = fence((late, keep_a, going_a, mlp_out, grad_second))
    came_a = swap(going_a, CORE)
    groups_b, keep_b, going_b, (own_b,) = mlp_call(late, True)
    came_a, keep_b, going_b, own_b = fence((came_a, keep_b, going_b, own_b))
    came_b = swap(going_b, CORE)
    totals = [None] * pairs
    for groups, keep in ((groups_a, keep_a), (groups_b, keep_b)):
        for i, e in enumerate(groups):
            totals[e // 2] = keep[i]
    totals, came_b = fence((totals, came_b))

    sum_mlp = OuterSum(totals)
    upper, lower = slice(0, up_rows), slice(up_rows, 2 * up_rows)
    sum_mlp.relays()
    sum_mlp.prepare(link_masks()[-1], upper)
    output, grad_joined, grad_cq, grad_ckv, gain_two, keep_two, send_two = pl.pallas_call(
        functools.partial(third_kernel, (blocks, places_two, layout, dp_count, mirrors)),
        out_shape=(
            whole((row_count, width), bf16),
            whole((row_count, width), f32),
            whole((row_count, width), bf16),
            whole((coarse_rows, 2 * width), bf16),
            whole((8, width), f32),
            whole((pairs, rows_two, width), bf16),
            whole((pairs, rows_two, width), bf16),
        ),
        in_specs=[SMEM] + [VMEM] * 12 + [ANY] * len(arrays_two),
        out_specs=(VMEM,) * 5 + (ANY,) * 2,
        scratch_shapes=[
            wide[3],
            wide[3],
            pltpu.VMEM((row_count, width), bf16),
            pltpu.SemaphoreType.DMA((n_two + dp_count,)),
        ],
        compiler_params=params(32),
        cost_estimate=cost(1e9, 1e6),
        name="cross_attention_backward",
    )(ints, coarse_seg, gains, mlp_out, grad_second, own_b, came_a, came_b, joined, cotangent, crossed, cq, ckv, *arrays_two)
    state, grad_joined = fence((sum_mlp.state(), grad_joined))
    sum_mlp.put(state)

    sum_mlp.singles(upper)
    for mask in link_masks():
        sum_mlp.prepare(mask, lower)
    coarse_grad, grad_res, grad_att, gain_grads, keep_two, send_two = pl.pallas_call(
        functools.partial(third_part, (places_two, layout, dp_count, mirrors)),
        out_shape=(
            whole((coarse_rows, width), f32),
            whole((row_count, width), f32),
            whole((row_count, width), bf16),
            whole((8, width), f32),
            whole((pairs, rows_two, width), bf16),
            whole((pairs, rows_two, width), bf16),
        ),
        in_specs=[SMEM] + [VMEM] * 8 + [ANY] * (2 + len(arrays_two)),
        out_specs=(VMEM,) * 4 + (ANY,) * 2,
        scratch_shapes=[
            wide[0],
            wide[1],
            wide[2],
            wide[0],
            wide[1],
            wide[2],
            pltpu.VMEM((row_count, width), bf16),
            pltpu.SemaphoreType.DMA((n_two,)),
        ],
        input_output_aliases={9: 4, 10: 5},
        compiler_params=params(),
        cost_estimate=cost(1e9, 1e6),
        name="cross_attention_weights",
    )(
        ints, coarse_view, gains, gain_two, grad_joined, residual, attended, grad_cq, grad_ckv, keep_two, send_two, *arrays_two
    )

    state, grad_att, keep_two, send_two = fence((sum_mlp.state(), grad_att, keep_two, send_two))
    sum_mlp.put(state)

    sum_mlp.singles(lower)
    came_two = swap(send_two, CORE)
    def attention_back(first, last, held):
        count = last - first
        return pl.pallas_call(
            functools.partial(fourth_kernel, (blocks, first, last)),
            out_shape=whole((row_count, 3 * width), bf16),
            in_specs=[SMEM] + [VMEM] * 3 + [ANY] * len(held),
            out_specs=ANY,
            scratch_shapes=[pltpu.VMEM((row_count, PAIR), bf16)] * (3 * count)
            + [pltpu.VMEM((row_count, PAIR), f32)] * (2 * count)
            + [pltpu.SemaphoreType.DMA((3 * count,))],
            input_output_aliases={4: 0} if held else {},
            compiler_params=params(32),
            cost_estimate=cost(1e9, 1e6),
            name="self_attention_backward",
        )(ints, seg_row, grad_att, qkv, *held)

    inner_mlp = [InnerSum(sum_mlp.result(0).reshape(fsdp_count, up_part, width))]
    inner_mlp[0].step()
    grad_proj = attention_back(0, HEADS // 2, ())
    state, came_two, grad_proj, inner_mlp[0].came = fence((sum_mlp.state(), came_two, grad_proj, inner_mlp[0].came))
    sum_mlp.put(state)

    sum_two = OuterSum(keep_two, came_two)
    sum_two.relays()
    sum_two.singles(masks=link_masks()[-1:])
    inner_mlp.append(InnerSum(sum_mlp.result(1).reshape(fsdp_count, up_part, width)))
    inner_mlp[1].step()
    keep_one, send_one = pl.pallas_call(
        functools.partial(sixth_kernel, (dp_count, places_one, qkv_rows, mirrors)),
        out_shape=(
            whole((pairs, qkv_rows + 16, width), bf16),
            whole((pairs, qkv_rows + 16, width), bf16),
        ),
        in_specs=[SMEM] + [VMEM] * 4 + [ANY] * len(arrays_one),
        out_specs=(ANY,) * 2,
        scratch_shapes=[
            pltpu.VMEM((3 * width, width), bf16),
            pltpu.VMEM((3 * width, width), bf16),
            pltpu.VMEM((16, width), bf16),
            pltpu.SemaphoreType.DMA((len(arrays_one) + 2 * dp_count,)),
        ],
        compiler_params=params(),
        cost_estimate=cost(1e9, 1e6),
        name="self_attention_weights",
    )(ints, gains, gain_grads, blended, grad_proj, *arrays_one)
    state, keep_one, send_one, inner_mlp[1].came = fence((sum_two.state(), keep_one, send_one, inner_mlp[1].came))
    sum_two.put(state)

    sum_two.singles(masks=link_masks()[:-1])
    came_one = swap(send_one, CORE)
    base, going_tok = pl.pallas_call(
        functools.partial(fifth_kernel, (dp_count, blocks, places_one, qkv_rows, mirrors)),
        out_shape=(
            whole((row_count, width), f32),
            whole((row_count, width), bf16),
        ),
        in_specs=[SMEM, SMEM] + [VMEM] * 4 + [ANY] * len(arrays_one),
        out_specs=(VMEM,) * 2,
        scratch_shapes=[
            pltpu.VMEM((3 * width, width), bf16),
            pltpu.SemaphoreType.DMA((len(arrays_one),)),
        ],
        compiler_params=params(),
        cost_estimate=cost(1e9, 1e6),
        name="self_attention_input",
    )(ints, mix_weight, gains, blended, grad_res, grad_proj, *arrays_one)
    state, came_one, going_tok = fence((sum_two.state(), came_one, going_tok))
    sum_two.put(state)

    sum_one = OuterSum(keep_one, came_one)
    sum_one.relays()
    came_tok = swap(going_tok, CORE)
    placed = pl.pallas_call(
        functools.partial(place_kernel, (blocks, mirrors)),
        out_shape=whole((pairs, row_count, width), bf16),
        in_specs=[SMEM, SMEM] + [VMEM] * 2,
        out_specs=VMEM,
        compiler_params=params(32),
        cost_estimate=cost(1e9, 1e6),
        name="place_partner_gradients",
    )(ints, ints_near, going_tok, came_tok)
    mlp_parts = jnp.concatenate([inner_parts(inner) for inner in inner_mlp], axis=1)
    inner_mlp = InnerSum(mlp_parts)
    inner_mlp.finish()
    state, placed, mlp_came = fence((sum_one.state(), placed, inner_mlp.came))
    sum_one.put(state)
    inner_mlp.came = mlp_came

    sum_one.singles()
    sum_tok = OuterSum(placed)
    sum_tok.relays()
    two_sum = sum_two.result()
    two_parts = jnp.concatenate(
        [two_sum[first : first + size].reshape(fsdp_count, size // fsdp_count, width) for first, size in layout], axis=1
    )
    inner_two = InnerSum(two_parts)
    inner_two.step()
    state, state_tok, two_came = fence((sum_one.state(), sum_tok.state(), inner_two.came))
    sum_one.put(state)
    sum_tok.put(state_tok)
    inner_two.came = two_came

    sum_tok.singles()
    one_sum = sum_one.result()
    gain_sum = jnp.broadcast_to(one_sum[qkv_rows : qkv_rows + 8][None], (fsdp_count, 8, width))
    one_parts = jnp.concatenate([one_sum[:qkv_rows].reshape(fsdp_count, qkv_part, width), gain_sum], axis=1)
    inner_one = InnerSum(one_parts)
    inner_one.step()
    one_mine = inner_one.result()
    mlp_mine = inner_mlp.result()
    up_shard, down_shard = mlp_mine[:up_part].T, mlp_mine[up_part:]
    two_mine = inner_two.result()
    found = []
    at = 0
    for size in sizes_two:
        found.append(two_mine[at : at + size])
        at += size
    ckv_shard, out_shard, cq_shard, cout_shard = found[0].T, found[1], found[2], found[3]
    qkv_shard = one_mine[:qkv_part].T
    gain_mine = lax.dynamic_slice(one_mine[qkv_part:], (0, device_me * part), (3, part))
    token_grad = base + sum_tok.result()
    return (
        output,
        token_grad,
        coarse_grad,
        gain_mine[0],
        qkv_shard,
        out_shard,
        gain_mine[1],
        cq_shard,
        ckv_shard,
        cout_shard,
        gain_mine[2],
        up_shard,
        down_shard,
    )


def solution(mesh):
    rows = P(("dp", "fsdp"), None)
    columns = P(None, ("dp", "fsdp"))
    line = P(("dp", "fsdp"))
    in_specs = (
        rows, rows, rows, rows, line, line, line, columns, rows,
        line, rows, columns, rows, line, columns, rows, rows,
    )
    out_specs = (
        rows, rows, rows, line, columns, rows, line, rows, columns, rows, line, columns, rows,
    )
    return jax.shard_map(shards, mesh=mesh, in_specs=in_specs, out_specs=out_specs, check_vma=False)
```

profile of v0, /device:TPU:0, one launch (start us, length us, event | category | flops | bytes accessed | tf_op | source)
XLA Modules:
  0.0 300.9 jit_solution(10759823962684091559)
XLA Ops:
  0.6 3.0 collective-permute-start
  13.7 3.2 %collective-permute-done.2 = bf16[128,768]{1,0:T(8,128)(2,1)S(1)} collective-permute-done((bf16[128,768]{1,0:T(8,128)(2,1)S(1)}, bf16[128,768]{1,0:T(8,128)(2,1)S(1)}, u32[]{:S(2)}, u32[]{:S(2)}) %collective-permute-start.2) | collective-permute-done | bytes 196640 | tf_op jit(solution)/shard_map/ppermute | solution.py:29
  16.9 6.9 %collective-permute-done.3 = bf16[128,768]{1,0:T(8,128)(2,1)S(1)} collective-permute-done((bf16[128,768]{1,0:T(8,128)(2,1)S(1)}, bf16[128,768]{1,0:T(8,128)(2,1)S(1)}, u32[]{:S(2)}, u32[]{:S(2)}) %collective-permute-start.3) | collective-permute-done | bytes 196640 | tf_op jit(solution)/shard_map/ppermute | solution.py:29
  26.6 4.7 %collective-permute-start.7 = (bf16[72,768]{1,0:T(8,128)(2,1)S(1)}, bf16[72,768]{1,0:T(8,128)(2,1)S(1)}, u32[]{:S(2)}, u32[]{:S(2)}) collective-permute-start(bf16[72,768]{1,0:T(8,128)(2,1)S(1)} %pad_maximum_fusion.14), channel_id=1, source_target_pairs={{0,1},{1,2},{2,3},{3,0},{4,5},{5,6},{6,7},{7,4},{8,9},{9,10},{10,1... | collective-permute-start | bytes 331784 | tf_op jit(solution)/shard_map/ppermute | solution.py:29
  36.3 3.5 %collective-permute-done.8 = bf16[72,768]{1,0:T(8,128)(2,1)S(1)} collective-permute-done((bf16[72,768]{1,0:T(8,128)(2,1)S(1)}, bf16[72,768]{1,0:T(8,128)(2,1)S(1)}, u32[]{:S(2)}, u32[]{:S(2)}) %collective-permute-start.8) | collective-permute-done | bytes 110624 | tf_op jit(solution)/shard_map/ppermute | solution.py:29
  45.3 7.1 %collective-permute-done.14 = bf16[192,768]{1,0:T(8,128)(2,1)S(1)} collective-permute-done((bf16[192,768]{1,0:T(8,128)(2,1)S(1)}, bf16[192,768]{1,0:T(8,128)(2,1)S(1)}, u32[]{:S(2)}, u32[]{:S(2)}) %collective-permute-start.14) | collective-permute-done | bytes 294944 | tf_op jit(solution)/shard_map/ppermute | solution.py:43
  56.0 7.3 %collective-permute-done.20 = bf16[2,40,768]{2,1,0:T(8,128)(2,1)S(1)} collective-permute-done((bf16[2,40,768]{2,1,0:T(8,128)(2,1)S(1)}, bf16[2,40,768]{2,1,0:T(8,128)(2,1)S(1)}, u32[]{:S(2)}, u32[]{:S(2)}) %collective-permute-start.20) | collective-permute-done | bytes 122912 | tf_op jit(solution)/shard_map/ppermute | solution.py:43
  71.3 12.5 %mix_self_attention.1 = (f32[512,768]{1,0:T(8,128)}, bf16[512,2304]{1,0:T(8,128)(2,1)}, bf16[512,768]{1,0:T(8,128)(2,1)}, f32[8,768]{1,0:T(8,128)}) custom-call(s32[17]{0:T(128)} %concatenate.78.ints, f32[4]{0:T(128)} %mix.3, s32[1,512]{1,0:T(1,128)} %seg_row.3, bf16[512,768]{1,0:T(8,128)(2,1)} %refs_0_, bf16[512,768]{1,0:T(8,128)(2,1)} %refs_0_, ...), custom_call_target="tpu_custom_call" | custom-call | flops 1000000000 | bytes 1000000 | tf_op jit(solution)/shard_map/mix_self_attention/pallas_call | solution.py:789
  83.8 2.9 collective-permute-done.24
  88.9 9.4 %collective-permute-done.30 = bf16[2,48,768]{2,1,0:T(8,128)(2,1)S(1)} collective-permute-done((bf16[2,48,768]{2,1,0:T(8,128)(2,1)S(1)}, bf16[2,48,768]{2,1,0:T(8,128)(2,1)S(1)}, u32[]{:S(2)}, u32[]{:S(2)}) %collective-permute-start.30) | collective-permute-done | bytes 147488 | tf_op jit(solution)/shard_map/ppermute | solution.py:43
  104.9 11.1 %cross_attention.1 = (f32[512,768]{1,0:T(8,128)}, bf16[512,768]{1,0:T(8,128)(2,1)}, bf16[128,1536]{1,0:T(8,128)(2,1)}, bf16[512,768]{1,0:T(8,128)(2,1)}, f32[512,768]{1,0:T(8,128)}, /*index=5*/bf16[512,768]{1,0:T(8,128)(2,1)}) custom-call(s32[17]{0:T(128)} %concatenate.78.ints, s32[1,128]{1,0:T(1,128)} %bitcast.170, bf16[128,768]{1,0:T(8,128)(2,1)} %coarse.3, ...), custom_call_target="tpu_custom_call" | custom-call | flops 1000000000 | bytes 1000000 | tf_op jit(solution)/shard_map/cross_attention/pallas_call | solution.py:830
  118.2 10.3 %collective-permute-done.31.refs_1_ = bf16[768,768]{1,0:T(8,128)(2,1)} collective-permute-done((bf16[768,768]{1,0:T(8,128)(2,1)S(1)}, bf16[768,768]{1,0:T(8,128)(2,1)}, u32[]{:S(2)}, u32[]{:S(2)}) %collective-permute-start.31) | collective-permute-done | bytes 1179680 | tf_op jit(solution)/shard_map/ppermute | solution.py:79
  130.9 16.2 %feed_forward.2 = (bf16[3,2,384,768]{3,2,1,0:T(8,128)(2,1)S(1)}, bf16[2,512,768]{2,1,0:T(8,128)(2,1)S(1)}, f32[512,768]{1,0:T(8,128)S(1)}, f32[512,768]{1,0:T(8,128)S(1)}) custom-call(bf16[512,768]{1,0:T(8,128)(2,1)S(1)} %copy-done.16, bf16[512,768]{1,0:T(8,128)(2,1)S(1)} %collective-permute-done.34.second_near, bf16[512,768]{1,0:T(8,128)(2,1)S(1)} %copy-done.3, ...), custom_call_target="tpu_custom_call" | custom-call | flops 1000000000 | bytes 1000000 | tf_op jit(solution)/shard_map/feed_forward/pallas_call | solution.py:869
  147.2 6.6 %feed_forward.3 = (bf16[1,2,384,768]{3,2,1,0:T(8,128)(2,1)S(1)}, bf16[2,512,768]{2,1,0:T(8,128)(2,1)S(1)}, bf16[2,512,768]{2,1,0:T(8,128)(2,1)S(1)}) custom-call(bf16[512,768]{1,0:T(8,128)(2,1)S(1)} %copy-done.16, bf16[512,768]{1,0:T(8,128)(2,1)S(1)} %collective-permute-done.34.second_near, bf16[512,768]{1,0:T(8,128)(2,1)S(1)} %copy-done.3, ...), custom_call_target="tpu_custom_call" | custom-call | flops 1000000000 | bytes 1000000 | tf_op jit(solution)/shard_map/feed_forward/pallas_call | solution.py:869
  158.4 13.3 %cross_attention_backward.1 = (bf16[512,768]{1,0:T(8,128)(2,1)}, f32[512,768]{1,0:T(8,128)S(1)}, bf16[512,768]{1,0:T(8,128)(2,1)S(1)}, bf16[128,1536]{1,0:T(8,12...) custom-call(s32[17]{0:T(128)S(1)} %copy-done.30, ...), custom_call_target="tpu_custom_call" | custom-call | flops 1000000000 | bytes 1000000 | tf_op jit(solution)/shard_map/cross_attention_backward/pallas_call | solution.py:906
  176.4 10.5 %cross_attention_weights.1 = (f32[128,768]{1,0:T(8,128)}, f32[512,768]{1,0:T(8,128)}, bf16[512,768]{1,0:T(8,128)(2,1)}, f32[8,768]{1,0:T(8,128)}, bf16[4,480,768...) custom-call(s32[17]{0:T(128)} %concatenate.78.ints, ...), custom_call_target="tpu_custom_call", output_to_operand_aliasing={{4}: (9, {}), {5}: (10, {})} | custom-call | flops 1000000000 | bytes 1000000 | tf_op jit(solution)/shard_map/cross_attention_weights/pallas_call | solution.py:935
  195.3 13.8 %self_attention_backward.1.grad_proj = bf16[512,2304]{1,0:T(8,128)(2,1)S(1)} custom-call(s32[17]{0:T(128)S(1)} %copy-done.31, s32[1,512]{1,0:T(1,128)S(1)} %copy-done.29, bf16[512,768]{1,0:T(8,128)(2,1)S(1)} %copy-done.24, bf16[512,2304]{1,0:T(8,128)(2,1)S(1)} %copy-done.17), custom_call_target="tpu_custom_call" | custom-call | flops 1000000000 | bytes 1000000 | tf_op jit(solution)/shard_map/self_attention_backward/pallas_call | solution.py:972
  216.9 8.3 %self_attention_weights.1 = (bf16[4,304,768]{2,1,0:T(8,128)(2,1)}, bf16[4,304,768]{2,1,0:T(8,128)(2,1)}) custom-call(s32[17]{0:T(128)} %concatenate.78.ints, f32[8,768]{1,0:T(8,128)} %get-tuple-element.226.gains, f32[8,768]{1,0:T(8,128)} %get-tuple-element.314.gain_grads, f32[512,768]{1,0:T(8,128)} %get-tuple-element.243.blended, bf16[512,2304]{1,0:T(8,128)(2,1)} %copy-done, ...), custom_call_target="tpu_custom_call" | custom-call | flops 1000000000 | bytes 1000000 | tf_op jit(solution)/shard_map/self_attention_weights/pallas_call | solution.py:997
  235.1 8.5 %self_attention_input.1 = (f32[512,768]{1,0:T(8,128)}, bf16[512,768]{1,0:T(8,128)(2,1)}) custom-call(s32[17]{0:T(128)} %concatenate.78.ints, f32[4]{0:T(128)} %mix.3, f32[8,768]{1,0:T(8,128)} %get-tuple-element.226.gains, f32[512,768]{1,0:T(8,128)} %get-tuple-element.243.blended, f32[512,768]{1,0:T(8,128)} %get-tuple-element.293.grad_res, ...), custom_call_target="tpu_custom_call" | custom-call | flops 1000000000 | bytes 1000000 | tf_op jit(solution)/shard_map/self_attention_input/pallas_call | solution.py:1020
  260.0 9.1 %collective-permute-done.57 = bf16[2,120,768]{2,1,0:T(8,128)(2,1)S(1)} collective-permute-done((bf16[2,120,768]{2,1,0:T(8,128)(2,1)S(1)}, bf16[2,120,768]{2,1,0:T(8,128)(2,1)S(1)}, u32[]{:S(2)}, u32[]{:S(2)}) %collective-permute-start.57) | collective-permute-done | bytes 368672 | tf_op jit(solution)/shard_map/ppermute | solution.py:43
  269.1 8.6 %collective-permute-done.55 = bf16[304,768]{1,0:T(8,128)(2,1)S(1)} collective-permute-done((bf16[304,768]{1,0:T(8,128)(2,1)S(1)}, bf16[304,768]{1,0:T(8,128)(2,1)S(1)}, u32[]{:S(2)}, u32[]{:S(2)}) %collective-permute-start.55) | collective-permute-done | bytes 466976 | tf_op jit(solution)/shard_map/ppermute | solution.py:79
  283.0 3.6 %collective-permute-done.62 = bf16[1,120,768]{2,1,0:T(8,128)(2,1)S(1)} collective-permute-done((bf16[1,120,768]{2,1,0:T(8,128)(2,1)S(1)}, bf16[1,120,768]{2,1,0:T(8,128)(2,1)S(1)}, u32[]{:S(2)}, u32[]{:S(2)}) %collective-permute-start.62) | collective-permute-done | bytes 184352 | tf_op jit(solution)/shard_map/ppermute | solution.py:43
  287.3 4.8 %collective-permute-done.60 = bf16[2,80,768]{2,1,0:T(8,128)(2,1)S(1)} collective-permute-done((bf16[2,80,768]{2,1,0:T(8,128)(2,1)S(1)}, bf16[2,80,768]{2,1,0:T(8,128)(2,1)S(1)}, u32[]{:S(2)}, u32[]{:S(2)}) %collective-permute-start.60) | collective-permute-done | bytes 245792 | tf_op jit(solution)/shard_map/ppermute | solution.py:43
  293.0 4.2 %collective-permute-done.61 = bf16[1,80,768]{2,1,0:T(8,128)(2,1)S(1)} collective-permute-done((bf16[1,80,768]{2,1,0:T(8,128)(2,1)S(1)}, bf16[1,80,768]{2,1,0:T(8,128)(2,1)S(1)}, u32[]{:S(2)}, u32[]{:S(2)}) %collective-permute-start.61) | collective-permute-done | bytes 122912 | tf_op jit(solution)/shard_map/ppermute | solution.py:43
  (344 shorter events, 109.1 us)
Async XLA Ops:
  0.6 23.2 %collective-permute-start = (bf16[512,768]{1,0:T(8,128)(2,1)}, bf16[512,768]{1,0:T(8,128)(2,1)S(1)}, u32[]{:S(2)}, u32[]{:S(2)}) collective-permute-start(bf16[512,768]{1,0:T(8,128)(2,1)} %refs_0_), channel_id=1, source_target_pairs={{0,8},{4,20},{8,0},{12,28},{16,24},{20,4},{24,16},{28,12},{1,9},{5... | collective-permute-start | bytes 2359304 | tf_op jit(solution)/shard_map/ppermute | solution.py:79
  3.6 21.2 %collective-permute-start.1 = (bf16[512,768]{1,0:T(8,128)(2,1)}, bf16[512,768]{1,0:T(8,128)(2,1)}, u32[]{:S(2)}, u32[]{:S(2)}) collective-permute-start(bf16[512,768]{1,0:T(8,128)(2,1)} %refs_0_), channel_id=1, source_target_pairs={{0,16},{4,12},{8,24},{12,4},{16,0},{20,28},{24,8},{28,20},{1,17},{... | collective-permute-start | bytes 2359304 | tf_op jit(solution)/shard_map/ppermute | solution.py:79
  65.5 18.3 %collective-permute-start.25 = (bf16[512,768]{1,0:T(8,128)(2,1)S(1)}, bf16[512,768]{1,0:T(8,128)(2,1)}, u32[]{:S(2)}, u32[]{:S(2)}) collective-permute-start(bf16[512,768]{1,0:T(8,128)(2,1)S(1)} %copy-done.3), channel_id=1, source_target_pairs={{0,4},{4,0},{8,12},{12,8},{16,20},{20,16},{24,28},{28,24},{1,5},{5... | collective-permute-start | bytes 2359304 | tf_op jit(solution)/shard_map/ppermute | solution.py:24
  66.5 20.3 %collective-permute-start.22 = (bf16[480,768]{1,0:T(8,128)(2,1)S(1)}, bf16[480,768]{1,0:T(8,128)(2,1)S(1)}, u32[]{:S(2)}, u32[]{:S(2)}) collective-permute-start(bf16[480,768]{1,0:T(8,128)(2,1)S(1)} %pad_maximum_fusion.2.refs_0_), channel_id=1, source_target_pairs={{0,8},{4,20},{8,0},{12,28},{16,24},{20,4},{24,16},{28,12},{1,9},{5... | collective-permute-start | bytes 2211848 | tf_op jit(solution)/shard_map/ppermute | solution.py:79
  67.4 19.3 %collective-permute-start.23 = (bf16[480,768]{1,0:T(8,128)(2,1)S(1)}, bf16[480,768]{1,0:T(8,128)(2,1)S(1)}, u32[]{:S(2)}, u32[]{:S(2)}) collective-permute-start(bf16[480,768]{1,0:T(8,128)(2,1)S(1)} %pad_maximum_fusion.2.refs_0_), channel_id=1, source_target_pairs={{0,16},{4,12},{8,24},{12,4},{16,0},{20,28},{24,8},{28,20},{1,17},{... | collective-permute-start | bytes 2211848 | tf_op jit(solution)/shard_map/ppermute | solution.py:79
  69.2 17.6 %collective-permute-start.24 = (bf16[2,104,768]{2,1,0:T(8,128)(2,1)}, bf16[2,104,768]{2,1,0:T(8,128)(2,1)S(1)}, u32[]{:S(2)}, u32[]{:S(2)}) collective-permute-start(bf16[2,104,768]{2,1,0:T(8,128)(2,1)} %pad_maximum_fusion.8), channel_id=1, source_target_pairs={{0,2},{1,3},{2,0},{3,1},{4,6},{5,7},{6,4},{7,5},{8,10},{9,11},{10,... | collective-permute-start | bytes 958472 | tf_op jit(solution)/shard_map/ppermute | solution.py:43
  100.0 28.5 %collective-permute-start.31 = (bf16[768,768]{1,0:T(8,128)(2,1)S(1)}, bf16[768,768]{1,0:T(8,128)(2,1)}, u32[]{:S(2)}, u32[]{:S(2)}) collective-permute-start(bf16[768,768]{1,0:T(8,128)(2,1)S(1)} %pad_maximum_fusion.1.refs_0_), channel_id=1, source_target_pairs={{0,8},{4,20},{8,0},{12,28},{16,24},{20,4},{24,16},{28,12},{1,9},{5... | collective-permute-start | bytes 3538952 | tf_op jit(solution)/shard_map/ppermute | solution.py:79
  100.9 27.6 %collective-permute-start.32 = (bf16[768,768]{1,0:T(8,128)(2,1)S(1)}, bf16[768,768]{1,0:T(8,128)(2,1)}, u32[]{:S(2)}, u32[]{:S(2)}) collective-permute-start(bf16[768,768]{1,0:T(8,128)(2,1)S(1)} %pad_maximum_fusion.1.refs_0_), channel_id=1, source_target_pairs={{0,16},{4,12},{8,24},{12,4},{16,0},{20,28},{24,8},{28,20},{1,17},{... | collective-permute-start | bytes 3538952 | tf_op jit(solution)/shard_map/ppermute | solution.py:79
  128.5 18.6 %collective-permute-start.36 = (bf16[768,768]{1,0:T(8,128)(2,1)}, bf16[768,768]{1,0:T(8,128)(2,1)S(1)}, u32[]{:S(2)}, u32[]{:S(2)}) collective-permute-start(bf16[768,768]{1,0:T(8,128)(2,1)} %collective-permute-done.31.refs_1_), channel_id=1, source_target_pairs={{0,16},{4,12},{8,24},{12,4},{16,0},{20,28},{24,8},{28,20},{1,17},{... | collective-permute-start | bytes 3538952 | tf_op jit(solution)/shard_map/ppermute | solution.py:79
  157.5 16.2 %collective-permute-start.39 = (bf16[768,768]{1,0:T(8,128)(2,1)S(1)}, bf16[768,768]{1,0:T(8,128)(2,1)S(1)}, u32[]{:S(2)}, u32[]{:S(2)}) collective-permute-start(bf16[768,768]{1,0:T(8,128)(2,1)S(1)} %bitcast.172), channel_id=1, source_target_pairs={{0,16},{4,12},{8,24},{12,4},{16,0},{20,28},{24,8},{28,20},{1,17},{... | collective-permute-start | bytes 3538952 | tf_op jit(solution)/shard_map/ppermute | solution.py:79
  174.0 15.4 %collective-permute-start.40 = (bf16[384,768]{1,0:T(8,128)(2,1)S(1)}, bf16[384,768]{1,0:T(8,128)(2,1)}, u32[]{:S(2)}, u32[]{:S(2)}) collective-permute-start(bf16[384,768]{1,0:T(8,128)(2,1)S(1)} %get-tuple-element.371), channel_id=1, source_target_pairs={{0,8},{4,20},{8,0},{12,28},{16,24},{20,4},{24,16},{28,12},{1,9},{5... | collective-permute-start | bytes 1769480 | tf_op jit(solution)/shard_map/ppermute | solution.py:79
  190.2 20.5 %collective-permute-start.44 = (bf16[4,480,768]{2,1,0:T(8,128)(2,1)}, bf16[4,480,768]{2,1,0:T(8,128)(2,1)}, u32[]{:S(2)}, u32[]{:S(2)}) collective-permute-start(bf16[4,480,768]{2,1,0:T(8,128)(2,1)} %get-tuple-element.307), channel_id=1, source_target_pairs={{0,4},{4,0},{8,12},{12,8},{16,20},{20,16},{24,28},{28,24},{1,5},{5... | collective-permute-start | bytes 8847368 | tf_op jit(solution)/shard_map/ppermute | solution.py:24
  190.2 20.5 %collective-permute-start.42 = (bf16[384,768]{1,0:T(8,128)(2,1)S(1)}, bf16[384,768]{1,0:T(8,128)(2,1)S(1)}, u32[]{:S(2)}, u32[]{:S(2)}) collective-permute-start(bf16[384,768]{1,0:T(8,128)(2,1)S(1)} %get-tuple-element.305), channel_id=1, source_target_pairs={{0,8},{4,20},{8,0},{12,28},{16,24},{20,4},{24,16},{28,12},{1,9},{5... | collective-permute-start | bytes 1769480 | tf_op jit(solution)/shard_map/ppermute | solution.py:79
  191.4 19.4 %collective-permute-start.43 = (bf16[384,768]{1,0:T(8,128)(2,1)}, bf16[384,768]{1,0:T(8,128)(2,1)S(1)}, u32[]{:S(2)}, u32[]{:S(2)}) collective-permute-start(bf16[384,768]{1,0:T(8,128)(2,1)} %slice.262), channel_id=1, source_target_pairs={{0,16},{4,12},{8,24},{12,4},{16,0},{20,28},{24,8},{28,20},{1,17},{... | collective-permute-start | bytes 1769480 | tf_op jit(solution)/shard_map/ppermute | solution.py:79
  194.2 16.5 %collective-permute-start.45 = (bf16[2,96,768]{2,1,0:T(8,128)(2,1)S(1)}, bf16[2,96,768]{2,1,0:T(8,128)(2,1)S(1)}, u32[]{:S(2)}, u32[]{:S(2)}) collective-permute-start(bf16[2,96,768]{2,1,0:T(8,128)(2,1)S(1)} %fusion.10), channel_id=1, source_target_pairs={{0,2},{1,3},{2,0},{3,1},{4,6},{5,7},{6,4},{7,5},{8,10},{9,11},{10,... | collective-permute-start | bytes 884744 | tf_op jit(solution)/shard_map/ppermute | solution.py:43
  212.6 17.8 %collective-permute-start.46 = (bf16[480,768]{1,0:T(8,128)(2,1)S(1)}, bf16[480,768]{1,0:T(8,128)(2,1)}, u32[]{:S(2)}, u32[]{:S(2)}) collective-permute-start(bf16[480,768]{1,0:T(8,128)(2,1)S(1)} %get-tuple-element.358), channel_id=1, source_target_pairs={{0,16},{4,12},{8,24},{12,4},{16,0},{20,28},{24,8},{28,20},{1,17},{... | collective-permute-start | bytes 2211848 | tf_op jit(solution)/shard_map/ppermute | solution.py:79
  213.4 18.7 %collective-permute-start.47 = (bf16[480,768]{1,0:T(8,128)(2,1)S(1)}, bf16[480,768]{1,0:T(8,128)(2,1)}, u32[]{:S(2)}, u32[]{:S(2)}) collective-permute-start(bf16[480,768]{1,0:T(8,128)(2,1)S(1)} %get-tuple-element.357), channel_id=1, source_target_pairs={{0,16},{4,12},{8,24},{12,4},{16,0},{20,28},{24,8},{28,20},{1,17},{... | collective-permute-start | bytes 2211848 | tf_op jit(solution)/shard_map/ppermute | solution.py:79
  214.9 15.5 %collective-permute-start.48 = (bf16[2,96,768]{2,1,0:T(8,128)(2,1)S(1)}, bf16[2,96,768]{2,1,0:T(8,128)(2,1)S(1)}, u32[]{:S(2)}, u32[]{:S(2)}) collective-permute-start(bf16[2,96,768]{2,1,0:T(8,128)(2,1)S(1)} %fusion.11), channel_id=1, source_target_pairs={{0,2},{1,3},{2,0},{3,1},{4,6},{5,7},{6,4},{7,5},{8,10},{9,11},{10,... | collective-permute-start | bytes 884744 | tf_op jit(solution)/shard_map/ppermute | solution.py:43
  249.7 19.4 %collective-permute-start.57 = (bf16[2,120,768]{2,1,0:T(8,128)(2,1)S(1)}, bf16[2,120,768]{2,1,0:T(8,128)(2,1)S(1)}, u32[]{:S(2)}, u32[]{:S(2)}) collective-permute-start(bf16[2,120,768]{2,1,0:T(8,128)(2,1)S(1)} %fusion.9), channel_id=1, source_target_pairs={{0,2},{1,3},{2,0},{3,1},{4,6},{5,7},{6,4},{7,5},{8,10},{9,11},{10,... | collective-permute-start | bytes 1105928 | tf_op jit(solution)/shard_map/ppermute | solution.py:43
  255.6 22.1 %collective-permute-start.56 = (bf16[512,768]{1,0:T(8,128)(2,1)S(1)}, bf16[512,768]{1,0:T(8,128)(2,1)S(1)}, u32[]{:S(2)}, u32[]{:S(2)}) collective-permute-start(bf16[512,768]{1,0:T(8,128)(2,1)S(1)} %get-tuple-element.363), channel_id=1, source_target_pairs={{0,16},{4,12},{8,24},{12,4},{16,0},{20,28},{24,8},{28,20},{1,17},{... | collective-permute-start | bytes 2359304 | tf_op jit(solution)/shard_map/ppermute | solution.py:79
  256.9 20.8 %collective-permute-start.55 = (bf16[304,768]{1,0:T(8,128)(2,1)S(1)}, bf16[304,768]{1,0:T(8,128)(2,1)S(1)}, u32[]{:S(2)}, u32[]{:S(2)}) collective-permute-start(bf16[304,768]{1,0:T(8,128)(2,1)S(1)} %add_convert_fusion.6), channel_id=1, source_target_pairs={{0,16},{4,12},{8,24},{12,4},{16,0},{20,28},{24,8},{28,20},{1,17},{... | collective-permute-start | bytes 1400840 | tf_op jit(solution)/shard_map/ppermute | solution.py:79
  258.1 19.6 %collective-permute-start.54 = (bf16[304,768]{1,0:T(8,128)(2,1)S(1)}, bf16[304,768]{1,0:T(8,128)(2,1)S(1)}, u32[]{:S(2)}, u32[]{:S(2)}) collective-permute-start(bf16[304,768]{1,0:T(8,128)(2,1)S(1)} %add_convert_fusion.7), channel_id=1, source_target_pairs={{0,8},{4,20},{8,0},{12,28},{16,24},{20,4},{24,16},{28,12},{1,9},{5... | collective-permute-start | bytes 1400840 | tf_op jit(solution)/shard_map/ppermute | solution.py:79
  280.9 18.2 %collective-permute-start.58 = (bf16[512,768]{1,0:T(8,128)(2,1)S(1)}, bf16[512,768]{1,0:T(8,128)(2,1)S(1)}, u32[]{:S(2)}, u32[]{:S(2)}) collective-permute-start(bf16[512,768]{1,0:T(8,128)(2,1)S(1)} %add_convert_fusion), channel_id=1, source_target_pairs={{0,8},{4,20},{8,0},{12,28},{16,24},{20,4},{24,16},{28,12},{1,9},{5... | collective-permute-start | bytes 2359304 | tf_op jit(solution)/shard_map/ppermute | solution.py:79
  282.1 17.0 %collective-permute-start.59 = (bf16[512,768]{1,0:T(8,128)(2,1)S(1)}, bf16[512,768]{1,0:T(8,128)(2,1)S(1)}, u32[]{:S(2)}, u32[]{:S(2)}) collective-permute-start(bf16[512,768]{1,0:T(8,128)(2,1)S(1)} %get-tuple-element.349), channel_id=1, source_target_pairs={{0,16},{4,12},{8,24},{12,4},{16,0},{20,28},{24,8},{28,20},{1,17},{... | collective-permute-start | bytes 2359304 | tf_op jit(solution)/shard_map/ppermute | solution.py:79
  (105 other events, 875.8 us)
where the time goes:
time: 306 us; the launch traced here: 301 us
  Pallas kernels  102 us (33%)
  waiting for transfers between devices  98.5 us (32%)
  starting transfers between devices  58.2 us (19%)
  local copies, waits for them, and re-layouts  22.9 us (7%)
  other arithmetic  17.3 us (6%)
    ppermute x11, waiting for transfers between devices, inner_swap(): return lax.ppermute(values, 'fsdp', [(i, i ^ mask) for i in range(count)])  51.4 us
    ppermute x26, starting transfers between devices, step_along(): lax.ppermute(values, 'dp', [(i, i ^ (mirrored(mask) if i & CORE else mask...  29.8 us
    ppermute x26, waiting for transfers between devices, step_along(): lax.ppermute(values, 'dp', [(i, i ^ (mirrored(mask) if i & CORE else mask...  27.5 us
    pallas_call x2, Pallas kernels, mlp_call(): pl.pallas_call(functools.partial(mlp_kernel, (groups, tuple(((e, None) fo...  22.8 us
    ppermute x6, waiting for transfers between devices, shift(): lax.ppermute(values, 'fsdp', [(i, (i + step) % count) for i in range(coun...  16.1 us
    pallas_call x1, Pallas kernels, attention_back(): pl.pallas_call(functools.partial(fourth_kernel, (blocks, first, last)), o...  13.8 us
    pallas_call x1, Pallas kernels, shards(): pl.pallas_call(functools.partial(third_kernel, (blocks, places_two, layou...  13.3 us
    ppermute x6, starting transfers between devices, shift(): lax.ppermute(values, 'fsdp', [(i, (i + step) % count) for i in range(coun...  12.9 us
  transfers between devices with their start and end apart: 63, of which 25 were waited for; matrix products, arithmetic and copies ran while one was open for 9% of the time, Pallas kernels for 34%

commit v1 on v0

--- a/solution.py
+++ b/solution.py
@@ -897,7 +897,7 @@
     for groups, keep in ((groups_a, keep_a), (groups_b, keep_b)):
         for i, e in enumerate(groups):
             totals[e // 2] = keep[i]
-    totals, came_b = fence((totals, came_b))
+    came_b = fence(came_b)
 
     sum_mlp = OuterSum(totals)
     upper, lower = slice(0, up_rows), slice(up_rows, 2 * up_rows)
@@ -1069,6 +1069,11 @@
     sum_tok.put(state_tok)
     inner_two.came = two_came
 
+    for mask in link_masks():
+        sum_tok.prepare(mask)
+    state, state_tok, inner_two.came = fence((sum_one.state(), sum_tok.state(), inner_two.came))
+    sum_one.put(state)
+    sum_tok.put(state_tok)
     sum_tok.singles()
     one_sum = sum_one.result()
     gain_sum = jnp.broadcast_to(one_sum[qkv_rows : qkv_rows + 8][None], (fsdp_count, 8, width))

time: 306 us -> 306 us (level)
  transfers between devices with their start and end apart: 63 -> 63, of which waited for: 25 -> 24; matrix products, arithmetic and copies ran while one was open for 9% -> 9% of each run, Pallas kernels for 34% -> 34%
where the time goes in v1:
time: 306 us; the launch traced here: 300 us
  Pallas kernels  102 us (33%)
  waiting for transfers between devices  95.5 us (31%)
  starting transfers between devices  58.6 us (19%)
  local copies, waits for them, and re-layouts  25.1 us (8%)
  other arithmetic  17.3 us (6%)
    ppermute x11, waiting for transfers between devices, inner_swap(): return lax.ppermute(values, 'fsdp', [(i, i ^ mask) for i in range(count)])  51.7 us
    ppermute x26, starting transfers between devices, step_along(): lax.ppermute(values, 'dp', [(i, i ^ (mirrored(mask) if i & CORE else mask...  30 us
    ppermute x26, waiting for transfers between devices, step_along(): lax.ppermute(values, 'dp', [(i, i ^ (mirrored(mask) if i & CORE else mask...  25 us
    pallas_call x2, Pallas kernels, mlp_call(): pl.pallas_call(functools.partial(mlp_kernel, (groups, tuple(((e, None) fo...  22.8 us
    ppermute x6, waiting for transfers between devices, shift(): lax.ppermute(values, 'fsdp', [(i, (i + step) % count) for i in range(coun...  16.1 us
    pallas_call x1, Pallas kernels, attention_back(): pl.pallas_call(functools.partial(fourth_kernel, (blocks, first, last)), o...  13.8 us
    pallas_call x1, Pallas kernels, shards(): pl.pallas_call(functools.partial(third_kernel, (blocks, places_two, layou...  13.3 us
    ppermute x6, starting transfers between devices, shift(): lax.ppermute(values, 'fsdp', [(i, (i + step) % count) for i in range(coun...  12.9 us
  transfers between devices with their start and end apart: 63, of which 24 were waited for; matrix products, arithmetic and copies ran while one was open for 9% of the time, Pallas kernels for 34%

profile of v1, /device:TPU:0, one launch (start us, length us, event | category | flops | bytes accessed | tf_op | source)
XLA Modules:
  0.0 300.4 jit_solution(14001408416495440925)
XLA Ops:
  0.6 3.0 collective-permute-start
  13.7 3.2 %collective-permute-done.2 = bf16[128,768]{1,0:T(8,128)(2,1)S(1)} collective-permute-done((bf16[128,768]{1,0:T(8,128)(2,1)S(1)}, bf16[128,768]{1,0:T(8,128)(2,1)S(1)}, u32[]{:S(2)}, u32[]{:S(2)}) %collective-permute-start.2) | collective-permute-done | bytes 196640 | tf_op jit(solution)/shard_map/ppermute | solution.py:29
  16.9 6.9 %collective-permute-done.3 = bf16[128,768]{1,0:T(8,128)(2,1)S(1)} collective-permute-done((bf16[128,768]{1,0:T(8,128)(2,1)S(1)}, bf16[128,768]{1,0:T(8,128)(2,1)S(1)}, u32[]{:S(2)}, u32[]{:S(2)}) %collective-permute-start.3) | collective-permute-done | bytes 196640 | tf_op jit(solution)/shard_map/ppermute | solution.py:29
  26.6 4.7 %collective-permute-start.7 = (bf16[72,768]{1,0:T(8,128)(2,1)S(1)}, bf16[72,768]{1,0:T(8,128)(2,1)S(1)}, u32[]{:S(2)}, u32[]{:S(2)}) collective-permute-start(bf16[72,768]{1,0:T(8,128)(2,1)S(1)} %pad_maximum_fusion.14), channel_id=1, source_target_pairs={{0,1},{1,2},{2,3},{3,0},{4,5},{5,6},{6,7},{7,4},{8,9},{9,10},{10,1... | collective-permute-start | bytes 331784 | tf_op jit(solution)/shard_map/ppermute | solution.py:29
  36.3 3.5 %collective-permute-done.8 = bf16[72,768]{1,0:T(8,128)(2,1)S(1)} collective-permute-done((bf16[72,768]{1,0:T(8,128)(2,1)S(1)}, bf16[72,768]{1,0:T(8,128)(2,1)S(1)}, u32[]{:S(2)}, u32[]{:S(2)}) %collective-permute-start.8) | collective-permute-done | bytes 110624 | tf_op jit(solution)/shard_map/ppermute | solution.py:29
  45.3 7.1 %collective-permute-done.14 = bf16[192,768]{1,0:T(8,128)(2,1)S(1)} collective-permute-done((bf16[192,768]{1,0:T(8,128)(2,1)S(1)}, bf16[192,768]{1,0:T(8,128)(2,1)S(1)}, u32[]{:S(2)}, u32[]{:S(2)}) %collective-permute-start.14) | collective-permute-done | bytes 294944 | tf_op jit(solution)/shard_map/ppermute | solution.py:43
  56.0 7.3 %collective-permute-done.20 = bf16[2,40,768]{2,1,0:T(8,128)(2,1)S(1)} collective-permute-done((bf16[2,40,768]{2,1,0:T(8,128)(2,1)S(1)}, bf16[2,40,768]{2,1,0:T(8,128)(2,1)S(1)}, u32[]{:S(2)}, u32[]{:S(2)}) %collective-permute-start.20) | collective-permute-done | bytes 122912 | tf_op jit(solution)/shard_map/ppermute | solution.py:43
  71.3 12.5 %mix_self_attention.1 = (f32[512,768]{1,0:T(8,128)}, bf16[512,2304]{1,0:T(8,128)(2,1)}, bf16[512,768]{1,0:T(8,128)(2,1)}, f32[8,768]{1,0:T(8,128)}) custom-call(s32[17]{0:T(128)} %concatenate.78.ints, f32[4]{0:T(128)} %mix.3, s32[1,512]{1,0:T(1,128)} %seg_row.3, bf16[512,768]{1,0:T(8,128)(2,1)} %refs_0_, bf16[512,768]{1,0:T(8,128)(2,1)} %refs_0_, ...), custom_call_target="tpu_custom_call" | custom-call | flops 1000000000 | bytes 1000000 | tf_op jit(solution)/shard_map/mix_self_attention/pallas_call | solution.py:789
  83.8 2.9 collective-permute-done.24
  88.9 9.4 %collective-permute-done.30 = bf16[2,48,768]{2,1,0:T(8,128)(2,1)S(1)} collective-permute-done((bf16[2,48,768]{2,1,0:T(8,128)(2,1)S(1)}, bf16[2,48,768]{2,1,0:T(8,128)(2,1)S(1)}, u32[]{:S(2)}, u32[]{:S(2)}) %collective-permute-start.30) | collective-permute-done | bytes 147488 | tf_op jit(solution)/shard_map/ppermute | solution.py:43
  104.9 11.1 %cross_attention.1 = (f32[512,768]{1,0:T(8,128)}, bf16[512,768]{1,0:T(8,128)(2,1)}, bf16[128,1536]{1,0:T(8,128)(2,1)}, bf16[512,768]{1,0:T(8,128)(2,1)}, f32[512,768]{1,0:T(8,128)}, /*index=5*/bf16[512,768]{1,0:T(8,128)(2,1)}) custom-call(s32[17]{0:T(128)} %concatenate.78.ints, s32[1,128]{1,0:T(1,128)} %bitcast.173, bf16[128,768]{1,0:T(8,128)(2,1)} %coarse.3, ...), custom_call_target="tpu_custom_call" | custom-call | flops 1000000000 | bytes 1000000 | tf_op jit(solution)/shard_map/cross_attention/pallas_call | solution.py:830
  118.2 10.3 %collective-permute-done.31.refs_1_ = bf16[768,768]{1,0:T(8,128)(2,1)} collective-permute-done((bf16[768,768]{1,0:T(8,128)(2,1)S(1)}, bf16[768,768]{1,0:T(8,128)(2,1)}, u32[]{:S(2)}, u32[]{:S(2)}) %collective-permute-start.31) | collective-permute-done | bytes 1179680 | tf_op jit(solution)/shard_map/ppermute | solution.py:79
  130.9 16.2 %feed_forward.2 = (bf16[3,2,384,768]{3,2,1,0:T(8,128)(2,1)S(1)}, bf16[2,512,768]{2,1,0:T(8,128)(2,1)S(1)}, f32[512,768]{1,0:T(8,128)S(1)}, f32[512,768]{1,0:T(8,128)S(1)}) custom-call(bf16[512,768]{1,0:T(8,128)(2,1)S(1)} %copy-done.16, bf16[512,768]{1,0:T(8,128)(2,1)S(1)} %collective-permute-done.34.second_near, bf16[512,768]{1,0:T(8,128)(2,1)S(1)} %copy-done.3, ...), custom_call_target="tpu_custom_call" | custom-call | flops 1000000000 | bytes 1000000 | tf_op jit(solution)/shard_map/feed_forward/pallas_call | solution.py:869
  147.2 6.6 %feed_forward.3 = (bf16[1,2,384,768]{3,2,1,0:T(8,128)(2,1)S(1)}, bf16[2,512,768]{2,1,0:T(8,128)(2,1)S(1)}, bf16[2,512,768]{2,1,0:T(8,128)(2,1)S(1)}) custom-call(bf16[512,768]{1,0:T(8,128)(2,1)S(1)} %copy-done.16, bf16[512,768]{1,0:T(8,128)(2,1)S(1)} %collective-permute-done.34.second_near, bf16[512,768]{1,0:T(8,128)(2,1)S(1)} %copy-done.3, ...), custom_call_target="tpu_custom_call" | custom-call | flops 1000000000 | bytes 1000000 | tf_op jit(solution)/shard_map/feed_forward/pallas_call | solution.py:869
  158.9 13.3 %cross_attention_backward.1 = (bf16[512,768]{1,0:T(8,128)(2,1)}, f32[512,768]{1,0:T(8,128)S(1)}, bf16[512,768]{1,0:T(8,128)(2,1)S(1)}, bf16[128,1536]{1,0:T(8,12...) custom-call(s32[17]{0:T(128)S(1)} %copy-done.30, ...), custom_call_target="tpu_custom_call" | custom-call | flops 1000000000 | bytes 1000000 | tf_op jit(solution)/shard_map/cross_attention_backward/pallas_call | solution.py:906
  176.6 10.5 %cross_attention_weights.1 = (f32[128,768]{1,0:T(8,128)}, f32[512,768]{1,0:T(8,128)}, bf16[512,768]{1,0:T(8,128)(2,1)}, f32[8,768]{1,0:T(8,128)}, bf16[4,480,768...) custom-call(s32[17]{0:T(128)} %concatenate.78.ints, ...), custom_call_target="tpu_custom_call", output_to_operand_aliasing={{4}: (9, {}), {5}: (10, {})} | custom-call | flops 1000000000 | bytes 1000000 | tf_op jit(solution)/shard_map/cross_attention_weights/pallas_call | solution.py:935
  195.5 13.8 %self_attention_backward.1.grad_proj = bf16[512,2304]{1,0:T(8,128)(2,1)S(1)} custom-call(s32[17]{0:T(128)S(1)} %copy-done.31, s32[1,512]{1,0:T(1,128)S(1)} %copy-done.29, bf16[512,768]{1,0:T(8,128)(2,1)S(1)} %copy-done.24, bf16[512,2304]{1,0:T(8,128)(2,1)S(1)} %copy-done.17), custom_call_target="tpu_custom_call" | custom-call | flops 1000000000 | bytes 1000000 | tf_op jit(solution)/shard_map/self_attention_backward/pallas_call | solution.py:972
  216.6 8.3 %self_attention_weights.1 = (bf16[4,304,768]{2,1,0:T(8,128)(2,1)}, bf16[4,304,768]{2,1,0:T(8,128)(2,1)}) custom-call(s32[17]{0:T(128)} %concatenate.78.ints, f32[8,768]{1,0:T(8,128)} %get-tuple-element.229.gains, f32[8,768]{1,0:T(8,128)} %get-tuple-element.312.gain_grads, f32[512,768]{1,0:T(8,128)} %get-tuple-element.246.blended, bf16[512,2304]{1,0:T(8,128)(2,1)} %copy-done, ...), custom_call_target="tpu_custom_call" | custom-call | flops 1000000000 | bytes 1000000 | tf_op jit(solution)/shard_map/self_attention_weights/pallas_call | solution.py:997
  234.5 8.5 %self_attention_input.1 = (f32[512,768]{1,0:T(8,128)}, bf16[512,768]{1,0:T(8,128)(2,1)}) custom-call(s32[17]{0:T(128)} %concatenate.78.ints, f32[4]{0:T(128)} %mix.3, f32[8,768]{1,0:T(8,128)} %get-tuple-element.229.gains, f32[512,768]{1,0:T(8,128)} %get-tuple-element.246.blended, f32[512,768]{1,0:T(8,128)} %get-tuple-element.291.grad_res, ...), custom_call_target="tpu_custom_call" | custom-call | flops 1000000000 | bytes 1000000 | tf_op jit(solution)/shard_map/self_attention_input/pallas_call | solution.py:1020
  259.6 9.1 %collective-permute-done.57 = bf16[2,120,768]{2,1,0:T(8,128)(2,1)S(1)} collective-permute-done((bf16[2,120,768]{2,1,0:T(8,128)(2,1)S(1)}, bf16[2,120,768]{2,1,0:T(8,128)(2,1)S(1)}, u32[]{:S(2)}, u32[]{:S(2)}) %collective-permute-start.57) | collective-permute-done | bytes 368672 | tf_op jit(solution)/shard_map/ppermute | solution.py:43
  268.7 8.6 %collective-permute-done.55 = bf16[304,768]{1,0:T(8,128)(2,1)S(1)} collective-permute-done((bf16[304,768]{1,0:T(8,128)(2,1)S(1)}, bf16[304,768]{1,0:T(8,128)(2,1)S(1)}, u32[]{:S(2)}, u32[]{:S(2)}) %collective-permute-start.55) | collective-permute-done | bytes 466976 | tf_op jit(solution)/shard_map/ppermute | solution.py:79
  282.5 3.2 %collective-permute-done.62 = bf16[1,120,768]{2,1,0:T(8,128)(2,1)S(1)} collective-permute-done((bf16[1,120,768]{2,1,0:T(8,128)(2,1)S(1)}, bf16[1,120,768]{2,1,0:T(8,128)(2,1)S(1)}, u32[]{:S(2)}, u32[]{:S(2)}) %collective-permute-start.62) | collective-permute-done | bytes 184352 | tf_op jit(solution)/shard_map/ppermute | solution.py:43
  286.5 5.6 %collective-permute-done.60 = bf16[2,80,768]{2,1,0:T(8,128)(2,1)S(1)} collective-permute-done((bf16[2,80,768]{2,1,0:T(8,128)(2,1)S(1)}, bf16[2,80,768]{2,1,0:T(8,128)(2,1)S(1)}, u32[]{:S(2)}, u32[]{:S(2)}) %collective-permute-start.60) | collective-permute-done | bytes 245792 | tf_op jit(solution)/shard_map/ppermute | solution.py:43
  292.9 4.2 %collective-permute-done.61 = bf16[1,80,768]{2,1,0:T(8,128)(2,1)S(1)} collective-permute-done((bf16[1,80,768]{2,1,0:T(8,128)(2,1)S(1)}, bf16[1,80,768]{2,1,0:T(8,128)(2,1)S(1)}, u32[]{:S(2)}, u32[]{:S(2)}) %collective-permute-start.61) | collective-permute-done | bytes 122912 | tf_op jit(solution)/shard_map/ppermute | solution.py:43
  (344 shorter events, 108.3 us)
Async XLA Ops:
  0.6 23.2 %collective-permute-start = (bf16[512,768]{1,0:T(8,128)(2,1)}, bf16[512,768]{1,0:T(8,128)(2,1)S(1)}, u32[]{:S(2)}, u32[]{:S(2)}) collective-permute-start(bf16[512,768]{1,0:T(8,128)(2,1)} %refs_0_), channel_id=1, source_target_pairs={{0,8},{4,20},{8,0},{12,28},{16,24},{20,4},{24,16},{28,12},{1,9},{5... | collective-permute-start | bytes 2359304 | tf_op jit(solution)/shard_map/ppermute | solution.py:79
  3.6 21.2 %collective-permute-start.1 = (bf16[512,768]{1,0:T(8,128)(2,1)}, bf16[512,768]{1,0:T(8,128)(2,1)}, u32[]{:S(2)}, u32[]{:S(2)}) collective-permute-start(bf16[512,768]{1,0:T(8,128)(2,1)} %refs_0_), channel_id=1, source_target_pairs={{0,16},{4,12},{8,24},{12,4},{16,0},{20,28},{24,8},{28,20},{1,17},{... | collective-permute-start | bytes 2359304 | tf_op jit(solution)/shard_map/ppermute | solution.py:79
  65.5 18.3 %collective-permute-start.25 = (bf16[512,768]{1,0:T(8,128)(2,1)S(1)}, bf16[512,768]{1,0:T(8,128)(2,1)}, u32[]{:S(2)}, u32[]{:S(2)}) collective-permute-start(bf16[512,768]{1,0:T(8,128)(2,1)S(1)} %copy-done.3), channel_id=1, source_target_pairs={{0,4},{4,0},{8,12},{12,8},{16,20},{20,16},{24,28},{28,24},{1,5},{5... | collective-permute-start | bytes 2359304 | tf_op jit(solution)/shard_map/ppermute | solution.py:24
  66.5 20.3 %collective-permute-start.22 = (bf16[480,768]{1,0:T(8,128)(2,1)S(1)}, bf16[480,768]{1,0:T(8,128)(2,1)S(1)}, u32[]{:S(2)}, u32[]{:S(2)}) collective-permute-start(bf16[480,768]{1,0:T(8,128)(2,1)S(1)} %pad_maximum_fusion.2.refs_0_), channel_id=1, source_target_pairs={{0,8},{4,20},{8,0},{12,28},{16,24},{20,4},{24,16},{28,12},{1,9},{5... | collective-permute-start | bytes 2211848 | tf_op jit(solution)/shard_map/ppermute | solution.py:79
  67.4 19.3 %collective-permute-start.23 = (bf16[480,768]{1,0:T(8,128)(2,1)S(1)}, bf16[480,768]{1,0:T(8,128)(2,1)S(1)}, u32[]{:S(2)}, u32[]{:S(2)}) collective-permute-start(bf16[480,768]{1,0:T(8,128)(2,1)S(1)} %pad_maximum_fusion.2.refs_0_), channel_id=1, source_target_pairs={{0,16},{4,12},{8,24},{12,4},{16,0},{20,28},{24,8},{28,20},{1,17},{... | collective-permute-start | bytes 2211848 | tf_op jit(solution)/shard_map/ppermute | solution.py:79
  69.2 17.6 %collective-permute-start.24 = (bf16[2,104,768]{2,1,0:T(8,128)(2,1)}, bf16[2,104,768]{2,1,0:T(8,128)(2,1)S(1)}, u32[]{:S(2)}, u32[]{:S(2)}) collective-permute-start(bf16[2,104,768]{2,1,0:T(8,128)(2,1)} %pad_maximum_fusion.8), channel_id=1, source_target_pairs={{0,2},{1,3},{2,0},{3,1},{4,6},{5,7},{6,4},{7,5},{8,10},{9,11},{10,... | collective-permute-start | bytes 958472 | tf_op jit(solution)/shard_map/ppermute | solution.py:43
  100.0 28.5 %collective-permute-start.31 = (bf16[768,768]{1,0:T(8,128)(2,1)S(1)}, bf16[768,768]{1,0:T(8,128)(2,1)}, u32[]{:S(2)}, u32[]{:S(2)}) collective-permute-start(bf16[768,768]{1,0:T(8,128)(2,1)S(1)} %pad_maximum_fusion.1.refs_0_), channel_id=1, source_target_pairs={{0,8},{4,20},{8,0},{12,28},{16,24},{20,4},{24,16},{28,12},{1,9},{5... | collective-permute-start | bytes 3538952 | tf_op jit(solution)/shard_map/ppermute | solution.py:79
  100.9 27.6 %collective-permute-start.32 = (bf16[768,768]{1,0:T(8,128)(2,1)S(1)}, bf16[768,768]{1,0:T(8,128)(2,1)}, u32[]{:S(2)}, u32[]{:S(2)}) collective-permute-start(bf16[768,768]{1,0:T(8,128)(2,1)S(1)} %pad_maximum_fusion.1.refs_0_), channel_id=1, source_target_pairs={{0,16},{4,12},{8,24},{12,4},{16,0},{20,28},{24,8},{28,20},{1,17},{... | collective-permute-start | bytes 3538952 | tf_op jit(solution)/shard_map/ppermute | solution.py:79
  128.5 18.6 %collective-permute-start.36 = (bf16[768,768]{1,0:T(8,128)(2,1)}, bf16[768,768]{1,0:T(8,128)(2,1)S(1)}, u32[]{:S(2)}, u32[]{:S(2)}) collective-permute-start(bf16[768,768]{1,0:T(8,128)(2,1)} %collective-permute-done.31.refs_1_), channel_id=1, source_target_pairs={{0,16},{4,12},{8,24},{12,4},{16,0},{20,28},{24,8},{28,20},{1,17},{... | collective-permute-start | bytes 3538952 | tf_op jit(solution)/shard_map/ppermute | solution.py:79
  154.4 17.8 %collective-permute-start.39 = (bf16[768,768]{1,0:T(8,128)(2,1)S(1)}, bf16[768,768]{1,0:T(8,128)(2,1)S(1)}, u32[]{:S(2)}, u32[]{:S(2)}) collective-permute-start(bf16[768,768]{1,0:T(8,128)(2,1)S(1)} %bitcast.175), channel_id=1, source_target_pairs={{0,16},{4,12},{8,24},{12,4},{16,0},{20,28},{24,8},{28,20},{1,17},{... | collective-permute-start | bytes 3538952 | tf_op jit(solution)/shard_map/ppermute | solution.py:79
  173.8 15.6 %collective-permute-start.40 = (bf16[384,768]{1,0:T(8,128)(2,1)S(1)}, bf16[384,768]{1,0:T(8,128)(2,1)}, u32[]{:S(2)}, u32[]{:S(2)}) collective-permute-start(bf16[384,768]{1,0:T(8,128)(2,1)S(1)} %get-tuple-element.377), channel_id=1, source_target_pairs={{0,8},{4,20},{8,0},{12,28},{16,24},{20,4},{24,16},{28,12},{1,9},{5... | collective-permute-start | bytes 1769480 | tf_op jit(solution)/shard_map/ppermute | solution.py:79
  190.2 20.2 %collective-permute-start.44 = (bf16[4,480,768]{2,1,0:T(8,128)(2,1)}, bf16[4,480,768]{2,1,0:T(8,128)(2,1)}, u32[]{:S(2)}, u32[]{:S(2)}) collective-permute-start(bf16[4,480,768]{2,1,0:T(8,128)(2,1)} %get-tuple-element.305), channel_id=1, source_target_pairs={{0,4},{4,0},{8,12},{12,8},{16,20},{20,16},{24,28},{28,24},{1,5},{5... | collective-permute-start | bytes 8847368 | tf_op jit(solution)/shard_map/ppermute | solution.py:24
  190.2 20.2 %collective-permute-start.42 = (bf16[384,768]{1,0:T(8,128)(2,1)S(1)}, bf16[384,768]{1,0:T(8,128)(2,1)S(1)}, u32[]{:S(2)}, u32[]{:S(2)}) collective-permute-start(bf16[384,768]{1,0:T(8,128)(2,1)S(1)} %get-tuple-element.303), channel_id=1, source_target_pairs={{0,8},{4,20},{8,0},{12,28},{16,24},{20,4},{24,16},{28,12},{1,9},{5... | collective-permute-start | bytes 1769480 | tf_op jit(solution)/shard_map/ppermute | solution.py:79
  191.6 18.8 %collective-permute-start.43 = (bf16[384,768]{1,0:T(8,128)(2,1)}, bf16[384,768]{1,0:T(8,128)(2,1)S(1)}, u32[]{:S(2)}, u32[]{:S(2)}) collective-permute-start(bf16[384,768]{1,0:T(8,128)(2,1)} %slice.267), channel_id=1, source_target_pairs={{0,16},{4,12},{8,24},{12,4},{16,0},{20,28},{24,8},{28,20},{1,17},{... | collective-permute-start | bytes 1769480 | tf_op jit(solution)/shard_map/ppermute | solution.py:79
  194.4 16.0 %collective-permute-start.45 = (bf16[2,96,768]{2,1,0:T(8,128)(2,1)S(1)}, bf16[2,96,768]{2,1,0:T(8,128)(2,1)S(1)}, u32[]{:S(2)}, u32[]{:S(2)}) collective-permute-start(bf16[2,96,768]{2,1,0:T(8,128)(2,1)S(1)} %fusion.10), channel_id=1, source_target_pairs={{0,2},{1,3},{2,0},{3,1},{4,6},{5,7},{6,4},{7,5},{8,10},{9,11},{10,... | collective-permute-start | bytes 884744 | tf_op jit(solution)/shard_map/ppermute | solution.py:43
  212.3 17.8 %collective-permute-start.46 = (bf16[480,768]{1,0:T(8,128)(2,1)S(1)}, bf16[480,768]{1,0:T(8,128)(2,1)}, u32[]{:S(2)}, u32[]{:S(2)}) collective-permute-start(bf16[480,768]{1,0:T(8,128)(2,1)S(1)} %get-tuple-element.364), channel_id=1, source_target_pairs={{0,16},{4,12},{8,24},{12,4},{16,0},{20,28},{24,8},{28,20},{1,17},{... | collective-permute-start | bytes 2211848 | tf_op jit(solution)/shard_map/ppermute | solution.py:79
  213.1 18.7 %collective-permute-start.47 = (bf16[480,768]{1,0:T(8,128)(2,1)S(1)}, bf16[480,768]{1,0:T(8,128)(2,1)}, u32[]{:S(2)}, u32[]{:S(2)}) collective-permute-start(bf16[480,768]{1,0:T(8,128)(2,1)S(1)} %get-tuple-element.363), channel_id=1, source_target_pairs={{0,16},{4,12},{8,24},{12,4},{16,0},{20,28},{24,8},{28,20},{1,17},{... | collective-permute-start | bytes 2211848 | tf_op jit(solution)/shard_map/ppermute | solution.py:79
  214.6 15.5 %collective-permute-start.48 = (bf16[2,96,768]{2,1,0:T(8,128)(2,1)S(1)}, bf16[2,96,768]{2,1,0:T(8,128)(2,1)S(1)}, u32[]{:S(2)}, u32[]{:S(2)}) collective-permute-start(bf16[2,96,768]{2,1,0:T(8,128)(2,1)S(1)} %fusion.11), channel_id=1, source_target_pairs={{0,2},{1,3},{2,0},{3,1},{4,6},{5,7},{6,4},{7,5},{8,10},{9,11},{10,... | collective-permute-start | bytes 884744 | tf_op jit(solution)/shard_map/ppermute | solution.py:43
  249.4 19.4 %collective-permute-start.57 = (bf16[2,120,768]{2,1,0:T(8,128)(2,1)S(1)}, bf16[2,120,768]{2,1,0:T(8,128)(2,1)S(1)}, u32[]{:S(2)}, u32[]{:S(2)}) collective-permute-start(bf16[2,120,768]{2,1,0:T(8,128)(2,1)S(1)} %fusion.9), channel_id=1, source_target_pairs={{0,2},{1,3},{2,0},{3,1},{4,6},{5,7},{6,4},{7,5},{8,10},{9,11},{10,... | collective-permute-start | bytes 1105928 | tf_op jit(solution)/shard_map/ppermute | solution.py:43
  255.3 22.1 %collective-permute-start.56 = (bf16[512,768]{1,0:T(8,128)(2,1)S(1)}, bf16[512,768]{1,0:T(8,128)(2,1)S(1)}, u32[]{:S(2)}, u32[]{:S(2)}) collective-permute-start(bf16[512,768]{1,0:T(8,128)(2,1)S(1)} %get-tuple-element.369), channel_id=1, source_target_pairs={{0,16},{4,12},{8,24},{12,4},{16,0},{20,28},{24,8},{28,20},{1,17},{... | collective-permute-start | bytes 2359304 | tf_op jit(solution)/shard_map/ppermute | solution.py:79
  256.6 20.8 %collective-permute-start.55 = (bf16[304,768]{1,0:T(8,128)(2,1)S(1)}, bf16[304,768]{1,0:T(8,128)(2,1)S(1)}, u32[]{:S(2)}, u32[]{:S(2)}) collective-permute-start(bf16[304,768]{1,0:T(8,128)(2,1)S(1)} %add_convert_fusion.6), channel_id=1, source_target_pairs={{0,16},{4,12},{8,24},{12,4},{16,0},{20,28},{24,8},{28,20},{1,17},{... | collective-permute-start | bytes 1400840 | tf_op jit(solution)/shard_map/ppermute | solution.py:79
  257.8 19.6 %collective-permute-start.54 = (bf16[304,768]{1,0:T(8,128)(2,1)S(1)}, bf16[304,768]{1,0:T(8,128)(2,1)S(1)}, u32[]{:S(2)}, u32[]{:S(2)}) collective-permute-start(bf16[304,768]{1,0:T(8,128)(2,1)S(1)} %add_convert_fusion.7), channel_id=1, source_target_pairs={{0,8},{4,20},{8,0},{12,28},{16,24},{20,4},{24,16},{28,12},{1,9},{5... | collective-permute-start | bytes 1400840 | tf_op jit(solution)/shard_map/ppermute | solution.py:79
  280.5 18.2 %collective-permute-start.58 = (bf16[512,768]{1,0:T(8,128)(2,1)S(1)}, bf16[512,768]{1,0:T(8,128)(2,1)S(1)}, u32[]{:S(2)}, u32[]{:S(2)}) collective-permute-start(bf16[512,768]{1,0:T(8,128)(2,1)S(1)} %add_convert_fusion), channel_id=1, source_target_pairs={{0,8},{4,20},{8,0},{12,28},{16,24},{20,4},{24,16},{28,12},{1,9},{5... | collective-permute-start | bytes 2359304 | tf_op jit(solution)/shard_map/ppermute | solution.py:79
  281.7 17.0 %collective-permute-start.59 = (bf16[512,768]{1,0:T(8,128)(2,1)S(1)}, bf16[512,768]{1,0:T(8,128)(2,1)S(1)}, u32[]{:S(2)}, u32[]{:S(2)}) collective-permute-start(bf16[512,768]{1,0:T(8,128)(2,1)S(1)} %get-tuple-element.355), channel_id=1, source_target_pairs={{0,16},{4,12},{8,24},{12,4},{16,0},{20,28},{24,8},{28,20},{1,17},{... | collective-permute-start | bytes 2359304 | tf_op jit(solution)/shard_map/ppermute | solution.py:79
  (105 other events, 860.0 us)
